TPU v7x, 256 devices: a whole 4x4x8 slice. The times are simulated.
256 devices in a mesh: row: 16 (over x, z_lo, core), col: 16 (over y, z_hi).
Axes of the slice: x: 4, y: 4, z: 8 (z_hi: 4, z_lo: 2; z = z_hi * 2 + z_lo), core: 2. Of those that a mesh axis runs over, the one named last changes fastest.
Arguments:
- features: bfloat16 [262144, 256], P('col', 'row'), may hold values from -6 to 6
- adjacency: bfloat16 [16, 16, 192, 128, 128], P('row', 'col'), may hold values from -0.15625 to 0.15625
- tile_coords: int32 [16, 16, 192, 2], P('row', 'col'), may hold values from 0 to 127, as said below
- tile_counts: int32 [16, 16], P('row', 'col'), may hold values from 1 to 192, as said below
- weight: bfloat16 [256, 256], replicated, may hold values from -0.375 to 0.375
- bias_vector: float32 [256], replicated, may hold values from -3 to 3
Outputs:
- embedded: bfloat16 [262144, 256], P(('row', 'col'))
Inputs may be any that keep to these rules, and one draw needn't show every extreme that they name: `tile_coords`: live slots of one block name distinct tiles; the first entry is a tile row below 128, the second a tile column below 128; slots past the count hold 0 in both entries. `tile_counts`: every diagonal block (row block index equal to column block index) is full.
All inputs are finite; a program needn't handle non-finite values.
Results may differ from a plain program's by a relative error of at most 0.015.
Values may be sent and summed in bfloat16 or wider, within the bound.
No kernel may reach another device: no remote copies, remote signals or barrier semaphores. Data moves between devices by JAX's collectives and lax.ppermute only.
A program may use at most 128 MiB of HBM per device.

v0:
```python
import jax
import jax.numpy as jnp
from jax import lax
from jax.sharding import PartitionSpec as P

TR_DEV = 8
GROUP = 32


def aggregate(panel_rows, tile_block, place_block, live_count, row_tiles):
    tile_size = tile_block.shape[-1]
    running = jnp.zeros((row_tiles, tile_size, panel_rows.shape[-1]), jnp.float32)

    def add_group(group_index, totals):
        first_slot = (group_index * GROUP).astype(jnp.int32)
        tile_values = lax.dynamic_slice_in_dim(tile_block, first_slot, GROUP, 0)
        tile_place = lax.dynamic_slice_in_dim(place_block, first_slot, GROUP, 0)
        live_mask = first_slot + jnp.arange(GROUP, dtype=jnp.int32) < live_count
        source = jnp.take(panel_rows, tile_place[:, 1], axis=0)
        product = jnp.einsum(
            "gmn,gnf->gmf", tile_values, source, preferred_element_type=jnp.float32
        )
        product = jnp.where(live_mask[:, None, None], product, jnp.float32(0.0))
        return totals.at[tile_place[:, 0]].add(product)

    groups = tile_block.shape[0] // GROUP
    running = lax.fori_loop(0, groups, add_group, running)
    return running.reshape(row_tiles * tile_size, panel_rows.shape[-1])


def shards(features, adjacency, tile_coords, tile_counts, weight, bias_vector):
    gathered = lax.all_gather(features, "row", axis=1, tiled=True)
    tile_size = adjacency.shape[-1]
    feature_count = gathered.shape[1]
    source_tiles = gathered.reshape(gathered.shape[0] // tile_size, tile_size, feature_count)
    row_tiles = TR_DEV * lax.axis_size("col")
    tile_block = adjacency[0, 0]
    place_block = tile_coords[0, 0]
    live_count = tile_counts[0, 0]
    partial_sum = aggregate(source_tiles, tile_block, place_block, live_count, row_tiles)
    summed = lax.psum_scatter(
        partial_sum.astype(jnp.bfloat16), "col", scatter_dimension=0, tiled=True
    )
    mixed_rows = jnp.dot(summed, weight, preferred_element_type=jnp.float32) + bias_vector
    return jnp.maximum(mixed_rows, jnp.float32(0.0)).astype(jnp.bfloat16)


def solution(mesh):
    in_specs = (
        P("col", "row"),
        P("row", "col", None, None, None),
        P("row", "col", None, None),
        P("row", "col"),
        P(),
        P(),
    )
    out_specs = P(("row", "col"), None)
    return jax.shard_map(shards, mesh=mesh, in_specs=in_specs, out_specs=out_specs, check_vma=False)
```

profile of v0, /device:TPU:34, one launch (start us, length us, event | category | flops | bytes accessed | tf_op | source)
XLA Modules:
  0.0 340.3 jit_solution(12481082858329424690)
XLA Ops:
  6.5 0.0 copy-start
  6.5 0.0 all-gather.2.cloned.1.call-start
  6.5 0.7 all-gather.2.cloned.1.call-update
  7.3 0.0 reduce-scatter.2.cloned.1.call-start
  7.3 59.2 %all-gather.2.cloned.1.call-done = bf16[16384,256]{0,1:T(8,128)(2,1)} async-done(((bf16[16384,16]{0,1:T(8,128)(2,1)}), bf16[16384,256]{0,1:T(8,128)(2,1)}) %all-gather.2.cloned.1.call-update) | async-done | bytes 8388624 | tf_op jit(solution)/shard_map/all_gather | solution.py:32
  66.5 12.0 %copy.7 = bf16[16384,256]{1,0:T(8,128)(2,1)} copy(bf16[16384,256]{0,1:T(8,128)(2,1)} %all-gather.2.cloned.1.call-done) | data formatting | bytes 16777216 | tf_op jit(solution)/shard_map/all_gather | solution.py:32
  78.4 0.0 copy-start.1
  78.4 7.8 %broadcast_in_dim.56 = f32[128,128,256]{2,1,0:T(8,128)} broadcast(f32[]{:T(128)} %constant.69.clone.1), dimensions={} | broadcast | bytes 16777220 | tf_op jit(solution)/shard_map/broadcast_in_dim | solution.py:12
  86.3 0.0 copy-done.1
  86.3 114.2 %while.13 = (s32[]{:T(128)}, f32[128,128,256]{2,1,0:T(8,128)}, s32[192,2]{0,1:T(2,128)S(1)}, s32[]{:T(128)}, bf16[192,128,128]{2,1,0:T(8,128)(2,1)}, /*index=5*/...) while((s32[]{:T(128)}, f32[128,128,256]{2,1,0:T(8,128)}, ...), condition=%wide.region_2.3_spmd, body=%wide.region_0.2_spmd.sunk | while | flops 271582656 | bytes 24123172 | solution.py:27
  86.3 0.7 add_compare_fusion.2
  86.9 0.1 constant_dynamic-slice_fusion.2
  87.0 4.1 %gather_fusion = bf16[32,128,256]{2,1,0:T(8,128)(2,1)S(1)} fusion(bf16[128,128,256]{2,1,0:T(8,128)(2,1)} %get-tuple-element.195, s32[1024]{0:T(1024)S(1)} %pad_clamp_fusion.2), kind=kCustom, calls=%fused_computation.clone.1 | custom fusion | bytes 4194432 | tf_op jit(solution)/shard_map/while/body/eval_jaxpr/jit(_take)/gather | solution.py:19
  91.1 4.0 %convolution_select_fusion.2 = f32[32,128,256]{2,1,0:T(8,128)} fusion(bf16[32,128,256]{2,1,0:T(8,128)(2,1)S(1)} %gather_fusion, pred[32]{0:T(512)(128)(4,1)S(1)} %and_bitcast_fusion.2, pred[32]{0:T(512)(128)(4,1)S(1)} %add_compare_fusion.2, bf16[192,128,128]{2,1,0:T(8,128)(2,1)} %get-tuple-element.194, s32[]{:T(128)S(6)} %select_n.65), kind=kOutput, calls=%fused_computation.2.clone.1 | convolution fusion | flops 270532608 | bytes 7340100 | tf_op jit(solution)/shard_map/while/body/eval_jaxpr/gmn,gnf->gmf/dot_general | solution.py:20
  95.1 9.9 %scatter_fusion = f32[128,128,256]{2,1,0:T(8,128)} fusion(f32[128,128,256]{2,1,0:T(8,128)} %get-tuple-element.181, s32[32]{0:T(128)S(1)} %get-tuple-element.168, f32[32,128,256]{2,1,0:T(8,128)} %convolution_select_fusion.2), kind=kCustom, calls=%fused_computation.1.clone.1 | custom fusion | flops 1048576 | bytes 12583040 | tf_op jit(solution)/shard_map/while/body/eval_jaxpr/scatter-add | solution.py:24
  105.0 0.7 add_compare_fusion.2
  105.6 0.1 constant_dynamic-slice_fusion.2
  105.7 4.1 %gather_fusion = bf16[32,128,256]{2,1,0:T(8,128)(2,1)S(1)} fusion(bf16[128,128,256]{2,1,0:T(8,128)(2,1)} %get-tuple-element.195, s32[1024]{0:T(1024)S(1)} %pad_clamp_fusion.2), kind=kCustom, calls=%fused_computation.clone.1 | custom fusion | bytes 4194432 | tf_op jit(solution)/shard_map/while/body/eval_jaxpr/jit(_take)/gather | solution.py:19
  109.8 4.0 %convolution_select_fusion.2 = f32[32,128,256]{2,1,0:T(8,128)} fusion(bf16[32,128,256]{2,1,0:T(8,128)(2,1)S(1)} %gather_fusion, pred[32]{0:T(512)(128)(4,1)S(1)} %and_bitcast_fusion.2, pred[32]{0:T(512)(128)(4,1)S(1)} %add_compare_fusion.2, bf16[192,128,128]{2,1,0:T(8,128)(2,1)} %get-tuple-element.194, s32[]{:T(128)S(6)} %select_n.65), kind=kOutput, calls=%fused_computation.2.clone.1 | convolution fusion | flops 270532608 | bytes 7340100 | tf_op jit(solution)/shard_map/while/body/eval_jaxpr/gmn,gnf->gmf/dot_general | solution.py:20
  113.8 10.3 %scatter_fusion = f32[128,128,256]{2,1,0:T(8,128)} fusion(f32[128,128,256]{2,1,0:T(8,128)} %get-tuple-element.181, s32[32]{0:T(128)S(1)} %get-tuple-element.168, f32[32,128,256]{2,1,0:T(8,128)} %convolution_select_fusion.2), kind=kCustom, calls=%fused_computation.1.clone.1 | custom fusion | flops 1048576 | bytes 12583040 | tf_op jit(solution)/shard_map/while/body/eval_jaxpr/scatter-add | solution.py:24
  124.1 0.7 add_compare_fusion.2
  124.7 0.1 constant_dynamic-slice_fusion.2
  124.8 4.1 %gather_fusion = bf16[32,128,256]{2,1,0:T(8,128)(2,1)S(1)} fusion(bf16[128,128,256]{2,1,0:T(8,128)(2,1)} %get-tuple-element.195, s32[1024]{0:T(1024)S(1)} %pad_clamp_fusion.2), kind=kCustom, calls=%fused_computation.clone.1 | custom fusion | bytes 4194432 | tf_op jit(solution)/shard_map/while/body/eval_jaxpr/jit(_take)/gather | solution.py:19
  128.9 4.0 %convolution_select_fusion.2 = f32[32,128,256]{2,1,0:T(8,128)} fusion(bf16[32,128,256]{2,1,0:T(8,128)(2,1)S(1)} %gather_fusion, pred[32]{0:T(512)(128)(4,1)S(1)} %and_bitcast_fusion.2, pred[32]{0:T(512)(128)(4,1)S(1)} %add_compare_fusion.2, bf16[192,128,128]{2,1,0:T(8,128)(2,1)} %get-tuple-element.194, s32[]{:T(128)S(6)} %select_n.65), kind=kOutput, calls=%fused_computation.2.clone.1 | convolution fusion | flops 270532608 | bytes 7340100 | tf_op jit(solution)/shard_map/while/body/eval_jaxpr/gmn,gnf->gmf/dot_general | solution.py:20
  132.9 10.3 %scatter_fusion = f32[128,128,256]{2,1,0:T(8,128)} fusion(f32[128,128,256]{2,1,0:T(8,128)} %get-tuple-element.181, s32[32]{0:T(128)S(1)} %get-tuple-element.168, f32[32,128,256]{2,1,0:T(8,128)} %convolution_select_fusion.2), kind=kCustom, calls=%fused_computation.1.clone.1 | custom fusion | flops 1048576 | bytes 12583040 | tf_op jit(solution)/shard_map/while/body/eval_jaxpr/scatter-add | solution.py:24
  143.1 0.7 add_compare_fusion.2
  143.8 0.1 constant_dynamic-slice_fusion.2
  143.9 4.1 %gather_fusion = bf16[32,128,256]{2,1,0:T(8,128)(2,1)S(1)} fusion(bf16[128,128,256]{2,1,0:T(8,128)(2,1)} %get-tuple-element.195, s32[1024]{0:T(1024)S(1)} %pad_clamp_fusion.2), kind=kCustom, calls=%fused_computation.clone.1 | custom fusion | bytes 4194432 | tf_op jit(solution)/shard_map/while/body/eval_jaxpr/jit(_take)/gather | solution.py:19
  148.0 4.0 %convolution_select_fusion.2 = f32[32,128,256]{2,1,0:T(8,128)} fusion(bf16[32,128,256]{2,1,0:T(8,128)(2,1)S(1)} %gather_fusion, pred[32]{0:T(512)(128)(4,1)S(1)} %and_bitcast_fusion.2, pred[32]{0:T(512)(128)(4,1)S(1)} %add_compare_fusion.2, bf16[192,128,128]{2,1,0:T(8,128)(2,1)} %get-tuple-element.194, s32[]{:T(128)S(6)} %select_n.65), kind=kOutput, calls=%fused_computation.2.clone.1 | convolution fusion | flops 270532608 | bytes 7340100 | tf_op jit(solution)/shard_map/while/body/eval_jaxpr/gmn,gnf->gmf/dot_general | solution.py:20
  152.0 10.3 %scatter_fusion = f32[128,128,256]{2,1,0:T(8,128)} fusion(f32[128,128,256]{2,1,0:T(8,128)} %get-tuple-element.181, s32[32]{0:T(128)S(1)} %get-tuple-element.168, f32[32,128,256]{2,1,0:T(8,128)} %convolution_select_fusion.2), kind=kCustom, calls=%fused_computation.1.clone.1 | custom fusion | flops 1048576 | bytes 12583040 | tf_op jit(solution)/shard_map/while/body/eval_jaxpr/scatter-add | solution.py:24
  162.2 0.7 add_compare_fusion.2
  162.9 0.1 constant_dynamic-slice_fusion.2
  163.0 4.1 %gather_fusion = bf16[32,128,256]{2,1,0:T(8,128)(2,1)S(1)} fusion(bf16[128,128,256]{2,1,0:T(8,128)(2,1)} %get-tuple-element.195, s32[1024]{0:T(1024)S(1)} %pad_clamp_fusion.2), kind=kCustom, calls=%fused_computation.clone.1 | custom fusion | bytes 4194432 | tf_op jit(solution)/shard_map/while/body/eval_jaxpr/jit(_take)/gather | solution.py:19
  167.1 4.0 %convolution_select_fusion.2 = f32[32,128,256]{2,1,0:T(8,128)} fusion(bf16[32,128,256]{2,1,0:T(8,128)(2,1)S(1)} %gather_fusion, pred[32]{0:T(512)(128)(4,1)S(1)} %and_bitcast_fusion.2, pred[32]{0:T(512)(128)(4,1)S(1)} %add_compare_fusion.2, bf16[192,128,128]{2,1,0:T(8,128)(2,1)} %get-tuple-element.194, s32[]{:T(128)S(6)} %select_n.65), kind=kOutput, calls=%fused_computation.2.clone.1 | convolution fusion | flops 270532608 | bytes 7340100 | tf_op jit(solution)/shard_map/while/body/eval_jaxpr/gmn,gnf->gmf/dot_general | solution.py:20
  171.0 10.3 %scatter_fusion = f32[128,128,256]{2,1,0:T(8,128)} fusion(f32[128,128,256]{2,1,0:T(8,128)} %get-tuple-element.181, s32[32]{0:T(128)S(1)} %get-tuple-element.168, f32[32,128,256]{2,1,0:T(8,128)} %convolution_select_fusion.2), kind=kCustom, calls=%fused_computation.1.clone.1 | custom fusion | flops 1048576 | bytes 12583040 | tf_op jit(solution)/shard_map/while/body/eval_jaxpr/scatter-add | solution.py:24
  181.3 0.7 add_compare_fusion.2
  182.0 0.1 constant_dynamic-slice_fusion.2
  182.1 4.1 %gather_fusion = bf16[32,128,256]{2,1,0:T(8,128)(2,1)S(1)} fusion(bf16[128,128,256]{2,1,0:T(8,128)(2,1)} %get-tuple-element.195, s32[1024]{0:T(1024)S(1)} %pad_clamp_fusion.2), kind=kCustom, calls=%fused_computation.clone.1 | custom fusion | bytes 4194432 | tf_op jit(solution)/shard_map/while/body/eval_jaxpr/jit(_take)/gather | solution.py:19
  186.2 4.0 %convolution_select_fusion.2 = f32[32,128,256]{2,1,0:T(8,128)} fusion(bf16[32,128,256]{2,1,0:T(8,128)(2,1)S(1)} %gather_fusion, pred[32]{0:T(512)(128)(4,1)S(1)} %and_bitcast_fusion.2, pred[32]{0:T(512)(128)(4,1)S(1)} %add_compare_fusion.2, bf16[192,128,128]{2,1,0:T(8,128)(2,1)} %get-tuple-element.194, s32[]{:T(128)S(6)} %select_n.65), kind=kOutput, calls=%fused_computation.2.clone.1 | convolution fusion | flops 270532608 | bytes 7340100 | tf_op jit(solution)/shard_map/while/body/eval_jaxpr/gmn,gnf->gmf/dot_general | solution.py:20
  190.1 10.3 %scatter_fusion = f32[128,128,256]{2,1,0:T(8,128)} fusion(f32[128,128,256]{2,1,0:T(8,128)} %get-tuple-element.181, s32[32]{0:T(128)S(1)} %get-tuple-element.168, f32[32,128,256]{2,1,0:T(8,128)} %convolution_select_fusion.2), kind=kCustom, calls=%fused_computation.1.clone.1 | custom fusion | flops 1048576 | bytes 12583040 | tf_op jit(solution)/shard_map/while/body/eval_jaxpr/scatter-add | solution.py:24
  200.4 9.0 %convert_element_type.9 = bf16[128,128,256]{2,1,0:T(8,128)(2,1)} convert(f32[128,128,256]{2,1,0:T(8,128)} %get-tuple-element.114) | non-fusion elementwise | flops 4194304 | bytes 25165824 | tf_op jit(solution)/shard_map/convert_element_type | solution.py:42
  209.4 0.0 copy-start.2
  209.4 0.0 reduce-scatter.2.cloned.1.call-update
  209.5 121.8 %reduce-scatter.2.cloned.1.call-done = bf16[1024,256]{1,0:T(8,128)(2,1)} async-done(((bf16[16384,256]{1,0:T(8,128)(2,1)}), bf16[1024,256]{1,0:T(8,128)(2,1)}) %reduce-scatter.2.cloned.1.call-update) | async-done | bytes 524304 | tf_op jit(solution)/shard_map/reduce_scatter | solution.py:41
  331.3 0.0 copy-done
  331.3 0.0 copy-done.2
  331.3 2.1 fusion.9
  (18 shorter events, 0.2 us)
Async XLA Ops:
  6.5 324.7 %copy-start = (bf16[256,256]{1,0:T(8,128)(2,1)S(1)}, bf16[256,256]{1,0:T(8,128)(2,1)}, u32[]{:S(2)}) copy-start(bf16[256,256]{1,0:T(8,128)(2,1)} %param.12) | copy-start | bytes 393220
  6.5 59.9 %all-gather.2.cloned.1.call-start = ((), (), s32[]{:S(2)}) async-start(), calls=%async_computation.1 | async-start | bytes 8912896 | tf_op jit(solution)/shard_map/all_gather | solution.py:32
  7.3 324.0 %reduce-scatter.2.cloned.1.call-start = ((), (), s32[]{:S(2)}) async-start(), calls=%async_computation.2 | async-start | bytes 8912896 | tf_op jit(solution)/shard_map/reduce_scatter | solution.py:41
  78.4 7.8 %copy-start.1 = (s32[1,1,192,2]{2,3,1,0:T(2,128)S(1)}, s32[1,1,192,2]{2,3,1,0:T(2,128)}, u32[]{:S(2)}) copy-start(s32[1,1,192,2]{2,3,1,0:T(2,128)} %param.10) | copy-start | bytes 4612
  209.4 121.8 %copy-start.2 = (f32[256]{0:T(256)S(1)}, f32[256]{0:T(256)}, u32[]{:S(2)}) copy-start(f32[256]{0:T(256)} %param.13) | copy-start | bytes 3076
Sparse Core Ops, SparseCore 0:
  9.2 57.2 all-gather.1
  209.6 121.6 reduce-scatter.1
where the time goes:
time: 343 us; the launch traced here: 340 us
  waiting for transfers between devices  182 us (53%)
  other arithmetic  74.4 us (22%)
  local copies, waits for them, and re-layouts  44.6 us (13%)
  matrix products  25.9 us (8%)
  between operations  13.4 us (4%)
    reduce_scatter x1, waiting for transfers between devices, shards(): lax.psum_scatter(partial_sum.astype(jnp.bfloat16), 'col', scatter_dimensi...  122 us
    scatter-add x6, other arithmetic, add_group(): return totals.at[tile_place[:, 0]].add(product)  61.3 us
    all_gather x1, waiting for transfers between devices, shards(): gathered = lax.all_gather(features, 'row', axis=1, tiled=True)  59.2 us
    gather x6, local copies, waits for them, and re-layouts, add_group(): source = jnp.take(panel_rows, tile_place[:, 1], axis=0)  24.4 us
    dot_general x6, matrix products, add_group(): jnp.einsum('gmn,gnf->gmf', tile_values, source, preferred_element_type=jn...  23.8 us
    all_gather x1, local copies, waits for them, and re-layouts, shards(): gathered = lax.all_gather(features, 'row', axis=1, tiled=True)  12 us
    convert_element_type x1, other arithmetic, shards(): partial_sum.astype(jnp.bfloat16)  9.02 us
    broadcast_in_dim x1, local copies, waits for them, and re-layouts, aggregate(): jnp.zeros((row_tiles, tile_size, panel_rows.shape[-1]), jnp.float32)  7.83 us
  transfers between devices with their start and end apart: 2, of which 2 were waited for; matrix products, arithmetic and copies ran while one was open for 0% of the time, Pallas kernels for 0%

commit v1 on v0

v1 whole, which is shorter than its diff:
```python
import functools
import jax
import jax.numpy as jnp
from jax import lax
from jax.experimental import pallas as pl
from jax.experimental.pallas import tpu as pltpu
from jax.sharding import PartitionSpec as P

UNROLL = 8
PIECES = 5
SLICE = 16
LOTS = 4
VMEM_LIMIT = 58 * 2**20
X, Y, Z = 4, 4, 4


def tile_kernel(place_ref, count_ref, order_ref, *refs):
    sources, outs = refs[:-PIECES - 4], refs[-PIECES - 4:-4]
    total, x_ref, a_ref, sems = refs[-4:]
    *x_sources, a_source = sources[:x_ref.shape[0] // SLICE + 1]
    rows = total.shape[0] - 1
    slots, side = a_ref.shape[0], a_ref.shape[-1]
    lot = slots // LOTS
    x_copies = [
        pltpu.make_async_copy(source, x_ref.at[pl.ds(k * SLICE, SLICE)], sems.at[k])
        for k, source in enumerate(x_sources)
    ]
    a_copies = [
        pltpu.make_async_copy(
            a_source.at[pl.ds(k * lot, lot)], a_ref.at[pl.ds(k * lot, lot)], sems.at[len(x_sources) + k]
        )
        for k in range(LOTS)
    ]
    for copy in x_copies + a_copies:
        copy.start()

    def clear(i, c):
        total[i] = jnp.zeros(total.shape[1:], jnp.float32)
        return c

    lax.fori_loop(0, rows, clear, 0, unroll=4)
    count = count_ref[0]

    def add_tiles(group, c):
        products = []
        for u in range(UNROLL):
            slot = group * UNROLL + u
            row = jnp.where(slot < count, place_ref[0, slot], rows)
            nodes = pl.ds(pl.multiple_of(place_ref[1, slot] * side, side), side)
            product = lax.dot_general(
                x_ref[:, nodes], a_ref[slot], (((1,), (1,)), ((), ())), preferred_element_type=jnp.float32
            )
            products.append((row, product))
        for row, product in products:
            total[row] += product
        return c

    for copy in x_copies:
        copy.wait()
    groups = lot // UNROLL
    for k in range(LOTS):
        a_copies[k].wait()
        last = jnp.minimum(pl.cdiv(count, UNROLL), (k + 1) * groups)
        lax.fori_loop(k * groups, last, add_tiles, 0)
    per = rows // (Y * Z)
    step = 0
    for out in outs:
        for place in range(out.shape[0] // per):
            start = order_ref[step] * per
            step += 1
            for i in range(per):
                out[place * per + i] = total[start + i].astype(jnp.bfloat16)


def partial_pieces(place, count, order, xs, tiles, rows, *before):
    feat, side = sum(x.shape[0] for x in xs), tiles.shape[-1]
    smem = pl.BlockSpec(memory_space=pltpu.SMEM)
    vmem = pl.BlockSpec(memory_space=pltpu.VMEM)
    hbm = pl.BlockSpec(memory_space=pltpu.HBM)
    piece = lambda part: jax.ShapeDtypeStruct((rows // part, feat, side), jnp.bfloat16)
    return pl.pallas_call(
        tile_kernel,
        out_shape=[piece(4), piece(4), piece(8), piece(8), piece(4)],
        in_specs=[smem, smem, smem] + [hbm] * (len(xs) + 1) + [pl.BlockSpec(memory_space=pl.ANY)] * len(before),
        out_specs=[vmem] * PIECES,
        scratch_shapes=[
            pltpu.VMEM((rows + 1, feat, side), jnp.float32),
            pltpu.VMEM((feat, xs[0].shape[1]), jnp.bfloat16),
            pltpu.VMEM(tiles.shape, jnp.bfloat16),
            pltpu.SemaphoreType.DMA((len(xs) + LOTS,)),
        ],
        compiler_params=pltpu.CompilerParams(vmem_limit_bytes=VMEM_LIMIT),
        name="tile_sum",
    )(place, count, order, *xs, tiles, *before)


def along_y(step):
    return [(y * Z + z, ((y + step) % Y) * Z + z) for y in range(Y) for z in range(Z)]


def along_z(step):
    return [(y * Z + z, y * Z + (z + step) % Z) for y in range(Y) for z in range(Z)]


def add(*terms):
    out = terms[0].astype(jnp.float32)
    for term in terms[1:]:
        out = out + term.astype(jnp.float32)
    return out.astype(jnp.bfloat16)


def send(v, perm):
    return lax.ppermute(v, "col", perm)


def start_y(pieces):
    return send(pieces[2], along_y(1)), send(pieces[3], along_y(-1))


def relay_y(pieces, far):
    next_up, next_down = pieces[1], pieces[4]
    half = pieces[2].shape[0]
    up = jnp.concatenate([add(next_up[:half], far[0]), next_up[half:]])
    down = jnp.concatenate([next_down[:half], add(next_down[half:], far[1])])
    return up, down


def end_y(pieces, up, down):
    near_up, near_down = send(up, along_y(1)), send(down, along_y(-1))
    own = pieces[0]
    n = own.shape[0] // Z
    return [add(*(t[d * n:(d + 1) * n] for t in (own, near_up, near_down))) for d in range(Z)]


def sum_z(mine):
    return add(mine[0], *(send(mine[d], along_z(d)) for d in (1, 2, 3)))


def row_step(along_x, other_z, other_core):
    return [
        (r, (((r >> 2) + along_x) % X) * 4 + ((r & 3) ^ (2 * other_z) ^ other_core)) for r in range(4 * X)
    ]


def then(first, values):
    return lax.optimization_barrier((first, values))[1]


def shards(features, adjacency, tile_coords, tile_counts, weight, bias_vector):
    tiles = adjacency[0, 0]
    rows = 8 * lax.axis_size("col")
    place = tile_coords[0, 0].T
    count = tile_counts[0]
    me = lax.axis_index("col")
    y, z = me // Z, me % Z
    order = jnp.stack([
        ((y + dy) % Y) * Z + (z + dz) % Z
        for dy, dzs in ((0, range(4)), (1, range(4)), (2, (0, 1)), (2, (2, 3)), (3, range(4)))
        for dz in dzs
    ])
    kernel = lambda xs, *before: partial_pieces(place, count, order, xs, tiles, rows, *before)
    own = features.T
    weights = weight.reshape(lax.axis_size("row"), own.shape[0], -1)
    r = lax.axis_index("row")

    def product(hidden, steps):
        source = jnp.stack([((r // 4 + dx) % X) * 4 + ((r % 4) ^ (2 * dz) ^ core) for dx, dz, core in steps])
        w = weights[source].reshape(hidden.shape[1], -1)
        return jnp.einsum("tfm,fg->tmg", hidden, w, preferred_element_type=jnp.float32)

    get = lambda v, *step: lax.ppermute(v, "row", row_step(*step))
    swap = lambda vs: [get(v, 0, 0, 1) for v in vs]
    pair = get(own, 0, 1, 0)
    side = [get(own, 1, 0, 0), get(own, -1, 0, 0)]
    near = [own, pair]
    near += swap(near)
    pieces_a = kernel(near, *side)
    side += [get(pair, 1, 0, 0), get(pair, -1, 0, 0)]
    far_a = start_y(pieces_a)
    side = then(pieces_a, side)
    swapped = swap(side)
    relay_a = relay_y(pieces_a, far_a)
    pieces_b = kernel(side + swapped, *relay_a)
    side = then(swapped, side)
    far = [get(side[0], 1, 0, 0), get(side[3], -1, 0, 0)]
    mine_a = end_y(pieces_a, *relay_a)
    far_b = start_y(pieces_b)
    far = then(pieces_b, far)
    pieces_c = kernel(far + swap(far), *mine_a)
    hidden_a = sum_z(mine_a)
    far_c = start_y(pieces_c)
    relay_b = relay_y(pieces_b, far_b)
    mine_b = end_y(pieces_b, *relay_b)
    relay_c = relay_y(pieces_c, then(hidden_a, far_c))
    mine_c = end_y(pieces_c, *relay_c)
    hidden_b = sum_z(mine_b)
    hidden_c = sum_z(mine_c)
    on = lambda chunk: [(dx, dz, core) for core in range(2) for dx, dz in chunk]
    mixed = bias_vector + product(hidden_a, on([(0, 0), (0, 1)]))
    mixed = mixed + product(hidden_b, on([(-1, 0), (1, 0), (-1, 1), (1, 1)]))
    mixed = mixed + product(hidden_c, on([(2, 0), (2, 1)]))
    embedded = jnp.maximum(mixed, jnp.float32(0.0)).astype(jnp.bfloat16)
    return embedded.reshape(-1, embedded.shape[-1])


def solution(mesh):
    in_specs = (
        P("col", "row"),
        P("row", "col", None, None, None),
        P("row", "col", None, None),
        P("row", "col"),
        P(),
        P(),
    )
    out_specs = P(("row", "col"), None)
    return jax.shard_map(shards, mesh=mesh, in_specs=in_specs, out_specs=out_specs, check_vma=False)
```

time: 343 us -> 174 us (0.51)
  the two profiles are of different devices: /device:TPU:34 before, /device:TPU:64 now
where the time goes in v1:
time: 174 us
  waiting for transfers between devices  71.7 us (41%)
  starting transfers between devices  42.2 us (24%)
  Pallas kernels  30.5 us (18%)
  other arithmetic  12.5 us (7%)
  local copies, waits for them, and re-layouts  12 us (7%)
  matrix products  4.06 us (2%)
    ppermute x21, waiting for transfers between devices, send(): return lax.ppermute(v, 'col', perm)  62.8 us
    pallas_call x3, Pallas kernels, partial_pieces(): pl.pallas_call(tile_kernel, out_shape=[piece(4), piece(4), piece(8), piec...  30.5 us
    ppermute x21, starting transfers between devices, send(): return lax.ppermute(v, 'col', perm)  25.9 us
    ppermute x15, starting transfers between devices, shards(): get = lambda v, *step: lax.ppermute(v, 'row', row_step(*step))  16.3 us
    convert_element_type x10, other arithmetic, add(): return out.astype(jnp.bfloat16)  10.4 us
    ppermute x15, waiting for transfers between devices, shards(): get = lambda v, *step: lax.ppermute(v, 'row', row_step(*step))  8.93 us
    dot_general x3, matrix products, product(): jnp.einsum('tfm,fg->tmg', hidden, w, preferred_element_type=jnp.float32)  4.06 us
    unnamed x46, local copies, waits for them, and re-layouts  3.54 us
  transfers between devices with their start and end apart: 36, of which 13 were waited for; matrix products, arithmetic and copies ran while one was open for 13% of the time, Pallas kernels for 18%

profile of v1, /device:TPU:64, one launch (start us, length us, event | category | flops | bytes accessed | tf_op | source)
XLA Modules:
  0.0 174.2 jit_solution(9080241139376713916)
XLA Ops:
  0.0 1.9 %collective-permute-start = (bf16[16,16384]{1,0:T(8,128)(2,1)}, bf16[16,16384]{1,0:T(8,128)(2,1)S(1)}, u32[]{:S(2)}, u32[]{:S(2)}) collective-permute-start(bf16[16,16384]{1,0:T(8,128)(2,1)} %bitcast.68), channel_id=1, source_target_pairs={{0,32},{16,48},{32,0},{48,16},{64,96},{80,112},{96,64},{112,80},{1... | collective-permute-start | bytes 1572872 | tf_op jit(solution)/shard_map/ppermute | solution.py:171
  1.9 1.5 collective-permute-start.3
  3.4 1.7 %collective-permute-start.4 = (bf16[16,16384]{1,0:T(8,128)(2,1)}, bf16[16,16384]{1,0:T(8,128)(2,1)S(1)}, u32[]{:S(2)}, u32[]{:S(2)}) collective-permute-start(bf16[16,16384]{1,0:T(8,128)(2,1)} %bitcast.71), channel_id=1, source_target_pairs={{0,192},{16,208},{32,224},{48,240},{64,0},{80,16},{96,32},{112,48}... | collective-permute-start | bytes 1572872 | tf_op jit(solution)/shard_map/ppermute | solution.py:171
  5.2 8.9 %collective-permute-done.refs_1_ = bf16[16,16384]{1,0:T(8,128)(2,1)S(1)} collective-permute-done((bf16[16,16384]{1,0:T(8,128)(2,1)}, bf16[16,16384]{1,0:T(8,128)(2,1)S(1)}, u32[]{:S(2)}, u32[]{:S(2)}) %collective-permute-start) | collective-permute-done | bytes 524320 | tf_op jit(solution)/shard_map/ppermute | solution.py:171
  14.1 1.5 collective-permute-start.12
  15.6 1.7 %collective-permute-start.13 = (bf16[16,16384]{1,0:T(8,128)(2,1)S(1)}, bf16[16,16384]{1,0:T(8,128)(2,1)S(1)}, u32[]{:S(2)}, u32[]{:S(2)}) collective-permute-start(bf16[16,16384]{1,0:T(8,128)(2,1)S(1)} %collective-permute-done.refs_1_), channel_id=1, source_target_pairs={{0,192},{16,208},{32,224},{48,240},{64,0},{80,16},{96,32},{112,48}... | collective-permute-start | bytes 1572872 | tf_op jit(solution)/shard_map/ppermute | solution.py:171
  18.0 0.7 stack.124.order_ref
  18.7 0.7 copy-done.1
  19.6 9.5 %tile_sum.3 = (bf16[32,64,128]{2,1,0:T(8,128)(2,1)}, bf16[32,64,128]{2,1,0:T(8,128)(2,1)}, bf16[16,64,128]{2,1,0:T(8,128)(2,1)}, bf16[16,64,128]{2,1,0:T(8,128)(2,1)}, bf16[32,64,128]{2,1,0:T(8,128)(2,1)}) custom-call(s32[2,192]{1,0:T(2,128)} %bitcast.76, s32[1]{0:T(128)} %bitcast.59.count_ref, s32[16]{0:T(128)} %stack.124.order_ref, ...), custom_call_target="tpu_custom_call" | custom-call | tf_op jit(solution)/shard_map/tile_sum/pallas_call | solution.py:81
  29.3 1.0 slice.148
  30.2 1.0 slice.146
  31.2 2.1 %collective-permute-start.5 = (bf16[16,64,128]{2,1,0:T(8,128)(2,1)}, bf16[16,64,128]{2,1,0:T(8,128)(2,1)S(1)}, u32[]{:S(2)}, u32[]{:S(2)}) collective-permute-start(bf16[16,64,128]{2,1,0:T(8,128)(2,1)} %get-tuple-element.32), channel_id=1, source_target_pairs={{0,4},{1,5},{2,6},{3,7},{4,8},{5,9},{6,10},{7,11},{8,12},{9,13},{1... | collective-permute-start | bytes 786440 | tf_op jit(solution)/shard_map/ppermute | solution.py:113
  33.3 1.2 collective-permute-start.14
  34.6 0.4 collective-permute-start.16
  35.0 3.0 %collective-permute-done.7 = bf16[16,64,128]{2,1,0:T(8,128)(2,1)S(1)} collective-permute-done((bf16[16,64,128]{2,1,0:T(8,128)(2,1)}, bf16[16,64,128]{2,1,0:T(8,128)(2,1)S(1)}, u32[]{:S(2)}, u32[]{:S(2)}) %collective-permute-start.7) | collective-permute-done | bytes 262176 | tf_op jit(solution)/shard_map/ppermute | solution.py:113
  38.0 0.8 collective-permute-start.17
  38.8 1.0 add_convert_fusion.9
  39.8 1.4 collective-permute-done.5
  41.2 1.0 add_convert_fusion.10
  42.4 2.1 %collective-permute-start.6 = (bf16[32,64,128]{2,1,0:T(8,128)(2,1)S(1)}, bf16[32,64,128]{2,1,0:T(8,128)(2,1)}, u32[]{:S(2)}, u32[]{:S(2)}) collective-permute-start(bf16[32,64,128]{2,1,0:T(8,128)(2,1)S(1)} %pad_maximum_fusion.2.refs_9_), channel_id=1, source_target_pairs={{0,4},{1,5},{2,6},{3,7},{4,8},{5,9},{6,10},{7,11},{8,12},{9,13},{1... | collective-permute-start | bytes 1572872 | tf_op jit(solution)/shard_map/ppermute | solution.py:113
  44.5 0.8 copy-done.13
  45.3 0.8 copy-done.14
  46.2 4.9 %collective-permute-start.26 = (bf16[16,16384]{1,0:T(8,128)(2,1)S(1)}, bf16[16,16384]{1,0:T(8,128)(2,1)}, u32[]{:S(2)}, u32[]{:S(2)}) collective-permute-start(bf16[16,16384]{1,0:T(8,128)(2,1)S(1)} %collective-permute-done.13.refs_3_), channel_id=1, source_target_pairs={{0,192},{16,208},{32,224},{48,240},{64,0},{80,16},{96,32},{112,48}... | collective-permute-start | bytes 1572872 | tf_op jit(solution)/shard_map/ppermute | solution.py:171
  51.1 11.4 %tile_sum.4 = (bf16[32,128,128]{2,1,0:T(8,128)(2,1)}, bf16[32,128,128]{2,1,0:T(8,128)(2,1)}, bf16[16,128,128]{2,1,0:T(8,128)(2,1)}, bf16[16,128,128]{2,1,0:T(8,128)(2,1)}, bf16[32,128,128]{2,1,0:T(8,128)(2,1)}) custom-call(s32[2,192]{1,0:T(2,128)} %bitcast.77, s32[1]{0:T(128)} %bitcast.60.count_ref, s32[16]{0:T(128)} %stack.124.order_ref, ...), custom_call_target="tpu_custom_call" | custom-call | tf_op jit(solution)/shard_map/tile_sum/pallas_call | solution.py:81
  62.7 1.4 add_convert_fusion.20
  64.1 1.1 collective-permute-start.11
  65.5 3.4 %collective-permute-start.9 = (bf16[8,64,128]{2,1,0:T(8,128)(2,1)S(1)}, bf16[8,64,128]{2,1,0:T(8,128)(2,1)S(1)}, u32[]{:S(2)}, u32[]{:S(2)}) collective-permute-start(bf16[8,64,128]{2,1,0:T(8,128)(2,1)S(1)} %get-tuple-element.63.refs_6_), channel_id=1, source_target_pairs={{0,1},{1,2},{2,3},{3,0},{4,5},{5,6},{6,7},{7,4},{8,9},{9,10},{10,1... | collective-permute-start | bytes 393224 | tf_op jit(solution)/shard_map/ppermute | solution.py:113
  69.0 1.1 slice.164
  70.1 1.1 slice.162
  71.2 2.1 %collective-permute-start.18 = (bf16[16,128,128]{2,1,0:T(8,128)(2,1)}, bf16[16,128,128]{2,1,0:T(8,128)(2,1)S(1)}, u32[]{:S(2)}, u32[]{:S(2)}) collective-permute-start(bf16[16,128,128]{2,1,0:T(8,128)(2,1)} %get-tuple-element.41), channel_id=1, source_target_pairs={{0,4},{1,5},{2,6},{3,7},{4,8},{5,9},{6,10},{7,11},{8,12},{9,13},{1... | collective-permute-start | bytes 1572872 | tf_op jit(solution)/shard_map/ppermute | solution.py:113
  73.3 6.8 %collective-permute-done.11 = bf16[8,64,128]{2,1,0:T(8,128)(2,1)S(1)} collective-permute-done((bf16[8,64,128]{2,1,0:T(8,128)(2,1)S(1)}, bf16[8,64,128]{2,1,0:T(8,128)(2,1)S(1)}, u32[]{:S(2)}, u32[]{:S(2)}) %collective-permute-start.11) | collective-permute-done | bytes 131104 | tf_op jit(solution)/shard_map/ppermute | solution.py:113
  80.2 0.4 collective-permute-start.28
  80.6 2.7 %collective-permute-done.9 = bf16[8,64,128]{2,1,0:T(8,128)(2,1)S(1)} collective-permute-done((bf16[8,64,128]{2,1,0:T(8,128)(2,1)S(1)}, bf16[8,64,128]{2,1,0:T(8,128)(2,1)S(1)}, u32[]{:S(2)}, u32[]{:S(2)}) %collective-permute-start.9) | collective-permute-done | bytes 131104 | tf_op jit(solution)/shard_map/ppermute | solution.py:113
  83.3 1.8 %add_convert_fusion.17 = (bf16[8,64,128]{2,1,0:T(8,128)(2,1)S(1)}, bf16[8,64,128]{2,1,0:T(8,128)(2,1)}) fusion(bf16[8,64,128]{2,1,0:T(8,128)(2,1)S(1)} %collective-permute-done.11, bf16[8,64,128]{2,1,0:T(8,128)(2,1)S(1)} %collective-permute-done.10, bf16[8,64,128]{2,1,0:T(8,128)(2,1)S(1)} %collective-permute-done.9, ...), kind=kLoop, calls=%fused_computation.34 | loop fusion | flops 917504 | bytes 1048576 | tf_op jit(solution)/shard_map/convert_element_type | solution.py:109
  85.1 1.3 add_convert_fusion
  86.6 0.7 copy-done.17
  87.5 9.5 %tile_sum.5 = (bf16[32,64,128]{2,1,0:T(8,128)(2,1)}, bf16[32,64,128]{2,1,0:T(8,128)(2,1)}, bf16[16,64,128]{2,1,0:T(8,128)(2,1)}, bf16[16,64,128]{2,1,0:T(8,128)(2,1)}, bf16[32,64,128]{2,1,0:T(8,128)(2,1)}) custom-call(s32[2,192]{1,0:T(2,128)} %bitcast.78, s32[1]{0:T(128)} %bitcast.61.count_ref, s32[16]{0:T(128)} %stack.124.order_ref, ...), custom_call_target="tpu_custom_call" | custom-call | tf_op jit(solution)/shard_map/tile_sum/pallas_call | solution.py:81
  97.2 3.2 %collective-permute-start.30 = (bf16[16,64,128]{2,1,0:T(8,128)(2,1)}, bf16[16,64,128]{2,1,0:T(8,128)(2,1)S(1)}, u32[]{:S(2)}, u32[]{:S(2)}) collective-permute-start(bf16[16,64,128]{2,1,0:T(8,128)(2,1)} %get-tuple-element.51), channel_id=1, source_target_pairs={{0,12},{1,13},{2,14},{3,15},{4,0},{5,1},{6,2},{7,3},{8,4},{9,5},{1... | collective-permute-start | bytes 786440 | tf_op jit(solution)/shard_map/ppermute | solution.py:113
  101.0 1.0 slice.180
  102.0 1.0 slice.178
  102.9 4.8 %collective-permute-done.29 = bf16[16,64,128]{2,1,0:T(8,128)(2,1)S(1)} collective-permute-done((bf16[16,64,128]{2,1,0:T(8,128)(2,1)}, bf16[16,64,128]{2,1,0:T(8,128)(2,1)S(1)}, u32[]{:S(2)}, u32[]{:S(2)}) %collective-permute-start.29) | collective-permute-done | bytes 262176 | tf_op jit(solution)/shard_map/ppermute | solution.py:113
  107.7 8.3 %collective-permute-done.30 = bf16[16,64,128]{2,1,0:T(8,128)(2,1)S(1)} collective-permute-done((bf16[16,64,128]{2,1,0:T(8,128)(2,1)}, bf16[16,64,128]{2,1,0:T(8,128)(2,1)S(1)}, u32[]{:S(2)}, u32[]{:S(2)}) %collective-permute-start.30) | collective-permute-done | bytes 262176 | tf_op jit(solution)/shard_map/ppermute | solution.py:113
  116.0 1.0 add_convert_fusion.2
  117.0 0.8 pad_maximum_fusion.5
  117.9 1.5 collective-permute-start.32
  119.5 0.8 pad_maximum_fusion.4
  120.3 0.5 collective-permute-start.31
  120.9 9.2 %collective-permute-done.19 = bf16[32,128,128]{2,1,0:T(8,128)(2,1)S(1)} collective-permute-done((bf16[32,128,128]{2,1,0:T(8,128)(2,1)S(1)}, bf16[32,128,128]{2,1,0:T(8,128)(2,1)S(1)}, u32[]{:S(2)}, u32[]{:S(2)}) %collective-permute-start.19) | collective-permute-done | bytes 1048608 | tf_op jit(solution)/shard_map/ppermute | solution.py:113
  130.2 1.1 add_convert_fusion.7
  131.3 2.3 %collective-permute-start.24 = (bf16[8,128,128]{2,1,0:T(8,128)(2,1)}, bf16[8,128,128]{2,1,0:T(8,128)(2,1)}, u32[]{:S(2)}, u32[]{:S(2)}) collective-permute-start(bf16[8,128,128]{2,1,0:T(8,128)(2,1)} %get-tuple-element.58), channel_id=1, source_target_pairs={{0,3},{1,0},{2,1},{3,2},{4,7},{5,4},{6,5},{7,6},{8,11},{9,8},{10,9... | collective-permute-start | bytes 786440 | tf_op jit(solution)/shard_map/ppermute | solution.py:113
  133.6 3.6 %collective-permute-start.22 = (bf16[8,128,128]{2,1,0:T(8,128)(2,1)}, bf16[8,128,128]{2,1,0:T(8,128)(2,1)}, u32[]{:S(2)}, u32[]{:S(2)}) collective-permute-start(bf16[8,128,128]{2,1,0:T(8,128)(2,1)} %get-tuple-element.57), channel_id=1, source_target_pairs={{0,1},{1,2},{2,3},{3,0},{4,5},{5,6},{6,7},{7,4},{8,9},{9,10},{10,1... | collective-permute-start | bytes 786440 | tf_op jit(solution)/shard_map/ppermute | solution.py:113
  137.2 0.5 gather_fusion.2
  137.7 0.6 gather_fusion.1
  138.3 0.5 gather_fusion
  138.8 2.3 %collective-permute-done.31 = bf16[32,64,128]{2,1,0:T(8,128)(2,1)} collective-permute-done((bf16[32,64,128]{2,1,0:T(8,128)(2,1)}, bf16[32,64,128]{2,1,0:T(8,128)(2,1)}, u32[]{:S(2)}, u32[]{:S(2)}) %collective-permute-start.31) | collective-permute-done | bytes 524320 | tf_op jit(solution)/shard_map/ppermute | solution.py:113
  141.1 1.5 add_convert_fusion.15
  142.8 2.9 %collective-permute-start.34 = (bf16[8,64,128]{2,1,0:T(8,128)(2,1)S(1)}, bf16[8,64,128]{2,1,0:T(8,128)(2,1)S(1)}, u32[]{:S(2)}, u32[]{:S(2)}) collective-permute-start(bf16[8,64,128]{2,1,0:T(8,128)(2,1)S(1)} %get-tuple-element.62), channel_id=1, source_target_pairs={{0,2},{1,3},{2,0},{3,1},{4,6},{5,7},{6,4},{7,5},{8,10},{9,11},{10,... | collective-permute-start | bytes 393224 | tf_op jit(solution)/shard_map/ppermute | solution.py:113
  145.8 19.7 %collective-permute-done.24 = bf16[8,128,128]{2,1,0:T(8,128)(2,1)} collective-permute-done((bf16[8,128,128]{2,1,0:T(8,128)(2,1)}, bf16[8,128,128]{2,1,0:T(8,128)(2,1)}, u32[]{:S(2)}, u32[]{:S(2)}) %collective-permute-start.24) | collective-permute-done | bytes 262176 | tf_op jit(solution)/shard_map/ppermute | solution.py:113
  165.4 1.5 fusion.4
  167.0 1.1 collective-permute-done.35
  168.0 0.4 collective-permute-done.34
  168.4 3.2 %collective-permute-done.33 = bf16[8,64,128]{2,1,0:T(8,128)(2,1)S(1)} collective-permute-done((bf16[8,64,128]{2,1,0:T(8,128)(2,1)S(1)}, bf16[8,64,128]{2,1,0:T(8,128)(2,1)S(1)}, u32[]{:S(2)}, u32[]{:S(2)}) %collective-permute-start.33) | collective-permute-done | bytes 131104 | tf_op jit(solution)/shard_map/ppermute | solution.py:113
  171.6 1.4 fusion.8
  173.0 1.2 fusion.3
  (93 shorter events, 2.6 us)
Async XLA Ops:
  0.0 137.2 %copy-start = (bf16[256,256]{1,0:T(8,128)(2,1)S(1)}, bf16[256,256]{1,0:T(8,128)(2,1)}, u32[]{:S(2)}) copy-start(bf16[256,256]{1,0:T(8,128)(2,1)} %param.10) | copy-start | bytes 393220
  0.0 14.0 %collective-permute-start = (bf16[16,16384]{1,0:T(8,128)(2,1)}, bf16[16,16384]{1,0:T(8,128)(2,1)S(1)}, u32[]{:S(2)}, u32[]{:S(2)}) collective-permute-start(bf16[16,16384]{1,0:T(8,128)(2,1)} %bitcast.68), channel_id=1, source_target_pairs={{0,32},{16,48},{32,0},{48,16},{64,96},{80,112},{96,64},{112,80},{1... | collective-permute-start | bytes 1572872 | tf_op jit(solution)/shard_map/ppermute | solution.py:171
  1.9 13.6 %collective-permute-start.1 = (bf16[16,16384]{1,0:T(8,128)(2,1)}, bf16[16,16384]{1,0:T(8,128)(2,1)S(1)}, u32[]{:S(2)}, u32[]{:S(2)}) collective-permute-start(bf16[16,16384]{1,0:T(8,128)(2,1)} %bitcast.69), channel_id=1, source_target_pairs={{0,16},{16,0},{32,48},{48,32},{64,80},{80,64},{96,112},{112,96},{1... | collective-permute-start | bytes 1572872 | tf_op jit(solution)/shard_map/ppermute | solution.py:171
  1.9 16.7 %collective-permute-start.3 = (bf16[16,16384]{1,0:T(8,128)(2,1)}, bf16[16,16384]{1,0:T(8,128)(2,1)S(1)}, u32[]{:S(2)}, u32[]{:S(2)}) collective-permute-start(bf16[16,16384]{1,0:T(8,128)(2,1)} %bitcast.70), channel_id=1, source_target_pairs={{0,64},{16,80},{32,96},{48,112},{64,128},{80,144},{96,160},{112,17... | collective-permute-start | bytes 1572872 | tf_op jit(solution)/shard_map/ppermute | solution.py:171
  3.4 15.2 %collective-permute-start.4 = (bf16[16,16384]{1,0:T(8,128)(2,1)}, bf16[16,16384]{1,0:T(8,128)(2,1)S(1)}, u32[]{:S(2)}, u32[]{:S(2)}) collective-permute-start(bf16[16,16384]{1,0:T(8,128)(2,1)} %bitcast.71), channel_id=1, source_target_pairs={{0,192},{16,208},{32,224},{48,240},{64,0},{80,16},{96,32},{112,48}... | collective-permute-start | bytes 1572872 | tf_op jit(solution)/shard_map/ppermute | solution.py:171
  14.1 4.6 %copy-start.9 = (bf16[16,16384]{1,0:T(8,128)(2,1)}, bf16[16,16384]{1,0:T(8,128)(2,1)S(1)}, u32[]{:S(2)}) copy-start(bf16[16,16384]{1,0:T(8,128)(2,1)S(1)} %collective-permute-done.refs_1_) | copy-start | bytes 1572868
  14.1 4.6 %collective-permute-start.2 = (bf16[16,16384]{1,0:T(8,128)(2,1)S(1)}, bf16[16,16384]{1,0:T(8,128)(2,1)}, u32[]{:S(2)}, u32[]{:S(2)}) collective-permute-start(bf16[16,16384]{1,0:T(8,128)(2,1)S(1)} %collective-permute-done.refs_1_), channel_id=1, source_target_pairs={{0,16},{16,0},{32,48},{48,32},{64,80},{80,64},{96,112},{112,96},{1... | collective-permute-start | bytes 1572872 | tf_op jit(solution)/shard_map/ppermute | solution.py:171
  14.1 19.2 %collective-permute-start.12 = (bf16[16,16384]{1,0:T(8,128)(2,1)S(1)}, bf16[16,16384]{1,0:T(8,128)(2,1)S(1)}, u32[]{:S(2)}, u32[]{:S(2)}) collective-permute-start(bf16[16,16384]{1,0:T(8,128)(2,1)S(1)} %collective-permute-done.refs_1_), channel_id=1, source_target_pairs={{0,64},{16,80},{32,96},{48,112},{64,128},{80,144},{96,160},{112,17... | collective-permute-start | bytes 1572872 | tf_op jit(solution)/shard_map/ppermute | solution.py:171
  15.6 3.1 %copy-start.10 = (bf16[16,16384]{1,0:T(8,128)(2,1)}, bf16[16,16384]{1,0:T(8,128)(2,1)S(1)}, u32[]{:S(2)}) copy-start(bf16[16,16384]{1,0:T(8,128)(2,1)S(1)} %collective-permute-done.1.refs_2_) | copy-start | bytes 1572868
  15.6 17.7 %collective-permute-start.13 = (bf16[16,16384]{1,0:T(8,128)(2,1)S(1)}, bf16[16,16384]{1,0:T(8,128)(2,1)S(1)}, u32[]{:S(2)}, u32[]{:S(2)}) collective-permute-start(bf16[16,16384]{1,0:T(8,128)(2,1)S(1)} %collective-permute-done.refs_1_), channel_id=1, source_target_pairs={{0,192},{16,208},{32,224},{48,240},{64,0},{80,16},{96,32},{112,48}... | collective-permute-start | bytes 1572872 | tf_op jit(solution)/shard_map/ppermute | solution.py:171
  18.6 0.8 copy-start.1
  18.7 1.0 copy-start.2
  29.2 8.8 %collective-permute-start.7 = (bf16[16,64,128]{2,1,0:T(8,128)(2,1)}, bf16[16,64,128]{2,1,0:T(8,128)(2,1)S(1)}, u32[]{:S(2)}, u32[]{:S(2)}) collective-permute-start(bf16[16,64,128]{2,1,0:T(8,128)(2,1)} %get-tuple-element.34), channel_id=1, source_target_pairs={{0,12},{1,13},{2,14},{3,15},{4,0},{5,1},{6,2},{7,3},{8,4},{9,5},{1... | collective-permute-start | bytes 786440 | tf_op jit(solution)/shard_map/ppermute | solution.py:113
  31.2 10.0 %collective-permute-start.5 = (bf16[16,64,128]{2,1,0:T(8,128)(2,1)}, bf16[16,64,128]{2,1,0:T(8,128)(2,1)S(1)}, u32[]{:S(2)}, u32[]{:S(2)}) collective-permute-start(bf16[16,64,128]{2,1,0:T(8,128)(2,1)} %get-tuple-element.32), channel_id=1, source_target_pairs={{0,4},{1,5},{2,6},{3,7},{4,8},{5,9},{6,10},{7,11},{8,12},{9,13},{1... | collective-permute-start | bytes 786440 | tf_op jit(solution)/shard_map/ppermute | solution.py:113
  33.3 17.8 %copy-start.8 = (bf16[16,16384]{1,0:T(8,128)(2,1)}, bf16[16,16384]{1,0:T(8,128)(2,1)S(1)}, u32[]{:S(2)}) copy-start(bf16[16,16384]{1,0:T(8,128)(2,1)S(1)} %collective-permute-done.12.refs_2_) | copy-start | bytes 1572868
  33.3 17.8 %copy-start.7 = (bf16[16,16384]{1,0:T(8,128)(2,1)}, bf16[16,16384]{1,0:T(8,128)(2,1)S(1)}, u32[]{:S(2)}) copy-start(bf16[16,16384]{1,0:T(8,128)(2,1)S(1)} %collective-permute-done.13.refs_3_) | copy-start | bytes 1572868
  33.3 9.0 %collective-permute-start.14 = (bf16[16,16384]{1,0:T(8,128)(2,1)}, bf16[16,16384]{1,0:T(8,128)(2,1)S(1)}, u32[]{:S(2)}, u32[]{:S(2)}) collective-permute-start(bf16[16,16384]{1,0:T(8,128)(2,1)} %copy-done.1), channel_id=1, source_target_pairs={{0,16},{16,0},{32,48},{48,32},{64,80},{80,64},{96,112},{112,96},{1... | collective-permute-start | bytes 1572872 | tf_op jit(solution)/shard_map/ppermute | solution.py:171
  34.5 10.0 %collective-permute-start.15 = (bf16[16,16384]{1,0:T(8,128)(2,1)}, bf16[16,16384]{1,0:T(8,128)(2,1)S(1)}, u32[]{:S(2)}, u32[]{:S(2)}) collective-permute-start(bf16[16,16384]{1,0:T(8,128)(2,1)} %copy-done.2), channel_id=1, source_target_pairs={{0,16},{16,0},{32,48},{48,32},{64,80},{80,64},{96,112},{112,96},{1... | collective-permute-start | bytes 1572872 | tf_op jit(solution)/shard_map/ppermute | solution.py:171
  34.6 9.9 %collective-permute-start.16 = (bf16[16,16384]{1,0:T(8,128)(2,1)S(1)}, bf16[16,16384]{1,0:T(8,128)(2,1)S(1)}, u32[]{:S(2)}, u32[]{:S(2)}) collective-permute-start(bf16[16,16384]{1,0:T(8,128)(2,1)S(1)} %collective-permute-done.12.refs_2_), channel_id=1, source_target_pairs={{0,16},{16,0},{32,48},{48,32},{64,80},{80,64},{96,112},{112,96},{1... | collective-permute-start | bytes 1572872 | tf_op jit(solution)/shard_map/ppermute | solution.py:171
  38.0 6.5 %collective-permute-start.17 = (bf16[16,16384]{1,0:T(8,128)(2,1)S(1)}, bf16[16,16384]{1,0:T(8,128)(2,1)S(1)}, u32[]{:S(2)}, u32[]{:S(2)}) collective-permute-start(bf16[16,16384]{1,0:T(8,128)(2,1)S(1)} %collective-permute-done.13.refs_3_), channel_id=1, source_target_pairs={{0,16},{16,0},{32,48},{48,32},{64,80},{80,64},{96,112},{112,96},{1... | collective-permute-start | bytes 1572872 | tf_op jit(solution)/shard_map/ppermute | solution.py:171
  39.8 11.3 %copy-start.3 = (bf16[32,64,128]{2,1,0:T(8,128)(2,1)}, bf16[32,64,128]{2,1,0:T(8,128)(2,1)S(1)}, u32[]{:S(2)}) copy-start(bf16[32,64,128]{2,1,0:T(8,128)(2,1)S(1)} %pad_maximum_fusion.3.refs_10_) | copy-start | bytes 1572868
  41.2 21.4 %collective-permute-start.8 = (bf16[32,64,128]{2,1,0:T(8,128)(2,1)S(1)}, bf16[32,64,128]{2,1,0:T(8,128)(2,1)}, u32[]{:S(2)}, u32[]{:S(2)}) collective-permute-start(bf16[32,64,128]{2,1,0:T(8,128)(2,1)S(1)} %pad_maximum_fusion.3.refs_10_), channel_id=1, source_target_pairs={{0,12},{1,13},{2,14},{3,15},{4,0},{5,1},{6,2},{7,3},{8,4},{9,5},{1... | collective-permute-start | bytes 1572872 | tf_op jit(solution)/shard_map/ppermute | solution.py:113
  42.3 8.8 %copy-start.4 = (bf16[32,64,128]{2,1,0:T(8,128)(2,1)}, bf16[32,64,128]{2,1,0:T(8,128)(2,1)S(1)}, u32[]{:S(2)}) copy-start(bf16[32,64,128]{2,1,0:T(8,128)(2,1)S(1)} %pad_maximum_fusion.2.refs_9_) | copy-start | bytes 1572868
  42.3 8.8 %copy-start.11 = (bf16[16,16384]{1,0:T(8,128)(2,1)}, bf16[16,16384]{1,0:T(8,128)(2,1)S(1)}, u32[]{:S(2)}) copy-start(bf16[16,16384]{1,0:T(8,128)(2,1)S(1)} %collective-permute-done.14.refs_4_) | copy-start | bytes 1572868
  42.4 20.3 %collective-permute-start.6 = (bf16[32,64,128]{2,1,0:T(8,128)(2,1)S(1)}, bf16[32,64,128]{2,1,0:T(8,128)(2,1)}, u32[]{:S(2)}, u32[]{:S(2)}) collective-permute-start(bf16[32,64,128]{2,1,0:T(8,128)(2,1)S(1)} %pad_maximum_fusion.2.refs_9_), channel_id=1, source_target_pairs={{0,4},{1,5},{2,6},{3,7},{4,8},{5,9},{6,10},{7,11},{8,12},{9,13},{1... | collective-permute-start | bytes 1572872 | tf_op jit(solution)/shard_map/ppermute | solution.py:113
  44.5 6.7 %copy-start.12 = (bf16[16,16384]{1,0:T(8,128)(2,1)}, bf16[16,16384]{1,0:T(8,128)(2,1)S(1)}, u32[]{:S(2)}) copy-start(bf16[16,16384]{1,0:T(8,128)(2,1)S(1)} %collective-permute-done.15.refs_5_) | copy-start | bytes 1572868
  44.5 0.8 copy-start.13
  45.3 0.8 copy-start.14
  46.1 19.4 %collective-permute-start.25 = (bf16[16,16384]{1,0:T(8,128)(2,1)}, bf16[16,16384]{1,0:T(8,128)(2,1)}, u32[]{:S(2)}, u32[]{:S(2)}) collective-permute-start(bf16[16,16384]{1,0:T(8,128)(2,1)} %copy-done.1), channel_id=1, source_target_pairs={{0,64},{16,80},{32,96},{48,112},{64,128},{80,144},{96,160},{112,17... | collective-permute-start | bytes 1572872 | tf_op jit(solution)/shard_map/ppermute | solution.py:171
  46.2 16.5 %copy-start.16 = (bf16[32,64,128]{2,1,0:T(8,128)(2,1)S(1)}, bf16[32,64,128]{2,1,0:T(8,128)(2,1)}, u32[]{:S(2)}) copy-start(bf16[32,64,128]{2,1,0:T(8,128)(2,1)} %get-tuple-element.30) | copy-start | bytes 1572868
  46.2 25.0 %collective-permute-start.26 = (bf16[16,16384]{1,0:T(8,128)(2,1)S(1)}, bf16[16,16384]{1,0:T(8,128)(2,1)}, u32[]{:S(2)}, u32[]{:S(2)}) collective-permute-start(bf16[16,16384]{1,0:T(8,128)(2,1)S(1)} %collective-permute-done.13.refs_3_), channel_id=1, source_target_pairs={{0,192},{16,208},{32,224},{48,240},{64,0},{80,16},{96,32},{112,48}... | collective-permute-start | bytes 1572872 | tf_op jit(solution)/shard_map/ppermute | solution.py:171
  62.6 22.5 %collective-permute-start.20 = (bf16[16,128,128]{2,1,0:T(8,128)(2,1)}, bf16[16,128,128]{2,1,0:T(8,128)(2,1)S(1)}, u32[]{:S(2)}, u32[]{:S(2)}) collective-permute-start(bf16[16,128,128]{2,1,0:T(8,128)(2,1)} %get-tuple-element.43), channel_id=1, source_target_pairs={{0,12},{1,13},{2,14},{3,15},{4,0},{5,1},{6,2},{7,3},{8,4},{9,5},{1... | collective-permute-start | bytes 1572872 | tf_op jit(solution)/shard_map/ppermute | solution.py:113
  64.1 22.5 %copy-start.19 = (bf16[8,64,128]{2,1,0:T(8,128)(2,1)}, bf16[8,64,128]{2,1,0:T(8,128)(2,1)S(1)}, u32[]{:S(2)}) copy-start(bf16[8,64,128]{2,1,0:T(8,128)(2,1)S(1)} %get-tuple-element.63.refs_6_) | copy-start | bytes 393220
  64.1 22.5 %copy-start.20 = (bf16[8,64,128]{2,1,0:T(8,128)(2,1)}, bf16[8,64,128]{2,1,0:T(8,128)(2,1)S(1)}, u32[]{:S(2)}) copy-start(bf16[8,64,128]{2,1,0:T(8,128)(2,1)S(1)} %get-tuple-element.64.refs_8_) | copy-start | bytes 393220
  64.1 22.5 %copy-start.21 = (bf16[8,64,128]{2,1,0:T(8,128)(2,1)}, bf16[8,64,128]{2,1,0:T(8,128)(2,1)S(1)}, u32[]{:S(2)}) copy-start(bf16[8,64,128]{2,1,0:T(8,128)(2,1)S(1)} %get-tuple-element.65.refs_7_) | copy-start | bytes 393220
  64.1 15.9 %collective-permute-start.11 = (bf16[8,64,128]{2,1,0:T(8,128)(2,1)S(1)}, bf16[8,64,128]{2,1,0:T(8,128)(2,1)S(1)}, u32[]{:S(2)}, u32[]{:S(2)}) collective-permute-start(bf16[8,64,128]{2,1,0:T(8,128)(2,1)S(1)} %get-tuple-element.64.refs_8_), channel_id=1, source_target_pairs={{0,3},{1,0},{2,1},{3,2},{4,7},{5,4},{6,5},{7,6},{8,11},{9,8},{10,9... | collective-permute-start | bytes 393224 | tf_op jit(solution)/shard_map/ppermute | solution.py:113
  65.3 14.9 %collective-permute-start.10 = (bf16[8,64,128]{2,1,0:T(8,128)(2,1)S(1)}, bf16[8,64,128]{2,1,0:T(8,128)(2,1)S(1)}, u32[]{:S(2)}, u32[]{:S(2)}) collective-permute-start(bf16[8,64,128]{2,1,0:T(8,128)(2,1)S(1)} %get-tuple-element.65.refs_7_), channel_id=1, source_target_pairs={{0,2},{1,3},{2,0},{3,1},{4,6},{5,7},{6,4},{7,5},{8,10},{9,11},{10,... | collective-permute-start | bytes 393224 | tf_op jit(solution)/shard_map/ppermute | solution.py:113
  65.5 17.7 %collective-permute-start.9 = (bf16[8,64,128]{2,1,0:T(8,128)(2,1)S(1)}, bf16[8,64,128]{2,1,0:T(8,128)(2,1)S(1)}, u32[]{:S(2)}, u32[]{:S(2)}) collective-permute-start(bf16[8,64,128]{2,1,0:T(8,128)(2,1)S(1)} %get-tuple-element.63.refs_6_), channel_id=1, source_target_pairs={{0,1},{1,2},{2,3},{3,0},{4,5},{5,6},{6,7},{7,4},{8,9},{9,10},{10,1... | collective-permute-start | bytes 393224 | tf_op jit(solution)/shard_map/ppermute | solution.py:113
  71.2 29.2 %collective-permute-start.18 = (bf16[16,128,128]{2,1,0:T(8,128)(2,1)}, bf16[16,128,128]{2,1,0:T(8,128)(2,1)S(1)}, u32[]{:S(2)}, u32[]{:S(2)}) collective-permute-start(bf16[16,128,128]{2,1,0:T(8,128)(2,1)} %get-tuple-element.41), channel_id=1, source_target_pairs={{0,4},{1,5},{2,6},{3,7},{4,8},{5,9},{6,10},{7,11},{8,12},{9,13},{1... | collective-permute-start | bytes 1572872 | tf_op jit(solution)/shard_map/ppermute | solution.py:113
  80.1 6.5 %collective-permute-start.27 = (bf16[16,16384]{1,0:T(8,128)(2,1)}, bf16[16,16384]{1,0:T(8,128)(2,1)S(1)}, u32[]{:S(2)}, u32[]{:S(2)}) collective-permute-start(bf16[16,16384]{1,0:T(8,128)(2,1)} %collective-permute-done.25.refs_0_), channel_id=1, source_target_pairs={{0,16},{16,0},{32,48},{48,32},{64,80},{80,64},{96,112},{112,96},{1... | collective-permute-start | bytes 1572872 | tf_op jit(solution)/shard_map/ppermute | solution.py:171
  80.2 6.4 %collective-permute-start.28 = (bf16[16,16384]{1,0:T(8,128)(2,1)}, bf16[16,16384]{1,0:T(8,128)(2,1)S(1)}, u32[]{:S(2)}, u32[]{:S(2)}) collective-permute-start(bf16[16,16384]{1,0:T(8,128)(2,1)} %collective-permute-done.26.refs_1_), channel_id=1, source_target_pairs={{0,16},{16,0},{32,48},{48,32},{64,80},{80,64},{96,112},{112,96},{1... | collective-permute-start | bytes 1572872 | tf_op jit(solution)/shard_map/ppermute | solution.py:171
  85.1 15.3 %copy-start.5 = (bf16[32,128,128]{2,1,0:T(8,128)(2,1)S(1)}, bf16[32,128,128]{2,1,0:T(8,128)(2,1)}, u32[]{:S(2)}) copy-start(bf16[32,128,128]{2,1,0:T(8,128)(2,1)} %get-tuple-element.40) | copy-start | bytes 3145732
  86.5 34.5 %collective-permute-start.21 = (bf16[32,128,128]{2,1,0:T(8,128)(2,1)S(1)}, bf16[32,128,128]{2,1,0:T(8,128)(2,1)S(1)}, u32[]{:S(2)}, u32[]{:S(2)}) collective-permute-start(bf16[32,128,128]{2,1,0:T(8,128)(2,1)S(1)} %pad_maximum_fusion.1), channel_id=1, source_target_pairs={{0,12},{1,13},{2,14},{3,15},{4,0},{5,1},{6,2},{7,3},{8,4},{9,5},{1... | collective-permute-start | bytes 3145736 | tf_op jit(solution)/shard_map/ppermute | solution.py:113
  86.6 0.8 copy-start.17
  86.6 1.0 copy-start.18
  97.1 22.3 %copy-start.15 = (bf16[32,64,128]{2,1,0:T(8,128)(2,1)S(1)}, bf16[32,64,128]{2,1,0:T(8,128)(2,1)}, u32[]{:S(2)}) copy-start(bf16[32,64,128]{2,1,0:T(8,128)(2,1)} %get-tuple-element.49) | copy-start | bytes 1572868
  97.1 33.1 %copy-start.6 = (bf16[32,128,128]{2,1,0:T(8,128)(2,1)S(1)}, bf16[32,128,128]{2,1,0:T(8,128)(2,1)}, u32[]{:S(2)}) copy-start(bf16[32,128,128]{2,1,0:T(8,128)(2,1)} %get-tuple-element.39) | copy-start | bytes 3145732
  97.1 10.6 %collective-permute-start.29 = (bf16[16,64,128]{2,1,0:T(8,128)(2,1)}, bf16[16,64,128]{2,1,0:T(8,128)(2,1)S(1)}, u32[]{:S(2)}, u32[]{:S(2)}) collective-permute-start(bf16[16,64,128]{2,1,0:T(8,128)(2,1)} %get-tuple-element.50), channel_id=1, source_target_pairs={{0,4},{1,5},{2,6},{3,7},{4,8},{5,9},{6,10},{7,11},{8,12},{9,13},{1... | collective-permute-start | bytes 786440 | tf_op jit(solution)/shard_map/ppermute | solution.py:113
  97.2 18.8 %collective-permute-start.30 = (bf16[16,64,128]{2,1,0:T(8,128)(2,1)}, bf16[16,64,128]{2,1,0:T(8,128)(2,1)S(1)}, u32[]{:S(2)}, u32[]{:S(2)}) collective-permute-start(bf16[16,64,128]{2,1,0:T(8,128)(2,1)} %get-tuple-element.51), channel_id=1, source_target_pairs={{0,12},{1,13},{2,14},{3,15},{4,0},{5,1},{6,2},{7,3},{8,4},{9,5},{1... | collective-permute-start | bytes 786440 | tf_op jit(solution)/shard_map/ppermute | solution.py:113
  100.7 29.5 %collective-permute-start.19 = (bf16[32,128,128]{2,1,0:T(8,128)(2,1)S(1)}, bf16[32,128,128]{2,1,0:T(8,128)(2,1)S(1)}, u32[]{:S(2)}, u32[]{:S(2)}) collective-permute-start(bf16[32,128,128]{2,1,0:T(8,128)(2,1)S(1)} %pad_maximum_fusion), channel_id=1, source_target_pairs={{0,4},{1,5},{2,6},{3,7},{4,8},{5,9},{6,10},{7,11},{8,12},{9,13},{1... | collective-permute-start | bytes 3145736 | tf_op jit(solution)/shard_map/ppermute | solution.py:113
  117.0 56.0 %copy-start.22 = (f32[256]{0:T(256)S(1)}, f32[256]{0:T(256)}, u32[]{:S(2)}) copy-start(f32[256]{0:T(256)} %param.11) | copy-start | bytes 3076
  117.9 21.0 %collective-permute-start.32 = (bf16[32,64,128]{2,1,0:T(8,128)(2,1)}, bf16[32,64,128]{2,1,0:T(8,128)(2,1)}, u32[]{:S(2)}, u32[]{:S(2)}) collective-permute-start(bf16[32,64,128]{2,1,0:T(8,128)(2,1)} %pad_maximum_fusion.5), channel_id=1, source_target_pairs={{0,12},{1,13},{2,14},{3,15},{4,0},{5,1},{6,2},{7,3},{8,4},{9,5},{1... | collective-permute-start | bytes 1572872 | tf_op jit(solution)/shard_map/ppermute | solution.py:113
  120.3 20.8 %collective-permute-start.31 = (bf16[32,64,128]{2,1,0:T(8,128)(2,1)}, bf16[32,64,128]{2,1,0:T(8,128)(2,1)}, u32[]{:S(2)}, u32[]{:S(2)}) collective-permute-start(bf16[32,64,128]{2,1,0:T(8,128)(2,1)} %pad_maximum_fusion.4), channel_id=1, source_target_pairs={{0,4},{1,5},{2,6},{3,7},{4,8},{5,9},{6,10},{7,11},{8,12},{9,13},{1... | collective-permute-start | bytes 1572872 | tf_op jit(solution)/shard_map/ppermute | solution.py:113
  131.3 34.1 %collective-permute-start.24 = (bf16[8,128,128]{2,1,0:T(8,128)(2,1)}, bf16[8,128,128]{2,1,0:T(8,128)(2,1)}, u32[]{:S(2)}, u32[]{:S(2)}) collective-permute-start(bf16[8,128,128]{2,1,0:T(8,128)(2,1)} %get-tuple-element.58), channel_id=1, source_target_pairs={{0,3},{1,0},{2,1},{3,2},{4,7},{5,4},{6,5},{7,6},{8,11},{9,8},{10,9... | collective-permute-start | bytes 786440 | tf_op jit(solution)/shard_map/ppermute | solution.py:113
  133.6 31.8 %collective-permute-start.23 = (bf16[8,128,128]{2,1,0:T(8,128)(2,1)}, bf16[8,128,128]{2,1,0:T(8,128)(2,1)}, u32[]{:S(2)}, u32[]{:S(2)}) collective-permute-start(bf16[8,128,128]{2,1,0:T(8,128)(2,1)} %get-tuple-element.59), channel_id=1, source_target_pairs={{0,2},{1,3},{2,0},{3,1},{4,6},{5,7},{6,4},{7,5},{8,10},{9,11},{10,... | collective-permute-start | bytes 786440 | tf_op jit(solution)/shard_map/ppermute | solution.py:113
  133.6 31.8 %collective-permute-start.22 = (bf16[8,128,128]{2,1,0:T(8,128)(2,1)}, bf16[8,128,128]{2,1,0:T(8,128)(2,1)}, u32[]{:S(2)}, u32[]{:S(2)}) collective-permute-start(bf16[8,128,128]{2,1,0:T(8,128)(2,1)} %get-tuple-element.57), channel_id=1, source_target_pairs={{0,1},{1,2},{2,3},{3,0},{4,5},{5,6},{6,7},{7,4},{8,9},{9,10},{10,1... | collective-permute-start | bytes 786440 | tf_op jit(solution)/shard_map/ppermute | solution.py:113
  142.7 25.4 %collective-permute-start.35 = (bf16[8,64,128]{2,1,0:T(8,128)(2,1)S(1)}, bf16[8,64,128]{2,1,0:T(8,128)(2,1)S(1)}, u32[]{:S(2)}, u32[]{:S(2)}) collective-permute-start(bf16[8,64,128]{2,1,0:T(8,128)(2,1)S(1)} %get-tuple-element.61), channel_id=1, source_target_pairs={{0,3},{1,0},{2,1},{3,2},{4,7},{5,4},{6,5},{7,6},{8,11},{9,8},{10,9... | collective-permute-start | bytes 393224 | tf_op jit(solution)/shard_map/ppermute | solution.py:113
  142.8 25.6 %collective-permute-start.34 = (bf16[8,64,128]{2,1,0:T(8,128)(2,1)S(1)}, bf16[8,64,128]{2,1,0:T(8,128)(2,1)S(1)}, u32[]{:S(2)}, u32[]{:S(2)}) collective-permute-start(bf16[8,64,128]{2,1,0:T(8,128)(2,1)S(1)} %get-tuple-element.62), channel_id=1, source_target_pairs={{0,2},{1,3},{2,0},{3,1},{4,6},{5,7},{6,4},{7,5},{8,10},{9,11},{10,... | collective-permute-start | bytes 393224 | tf_op jit(solution)/shard_map/ppermute | solution.py:113
  165.4 6.2 %collective-permute-start.33 = (bf16[8,64,128]{2,1,0:T(8,128)(2,1)S(1)}, bf16[8,64,128]{2,1,0:T(8,128)(2,1)S(1)}, u32[]{:S(2)}, u32[]{:S(2)}) collective-permute-start(bf16[8,64,128]{2,1,0:T(8,128)(2,1)S(1)} %get-tuple-element.60), channel_id=1, source_target_pairs={{0,1},{1,2},{2,3},{3,0},{4,5},{5,6},{6,7},{7,4},{8,9},{9,10},{10,1... | collective-permute-start | bytes 393224 | tf_op jit(solution)/shard_map/ppermute | solution.py:113

commit v2 on v1

--- a/solution.py
+++ b/solution.py
@@ -7,15 +7,16 @@
 from jax.sharding import PartitionSpec as P
 
 UNROLL = 8
-PIECES = 5
+WHOLE = (4, 4, 4, 4)
+HALVED = (8,) * 8
 SLICE = 16
 LOTS = 4
-VMEM_LIMIT = 58 * 2**20
+VMEM_LIMIT = 46 * 2**20
 X, Y, Z = 4, 4, 4
 
 
-def tile_kernel(place_ref, count_ref, order_ref, *refs):
-    sources, outs = refs[:-PIECES - 4], refs[-PIECES - 4:-4]
+def tile_kernel(pieces, place_ref, count_ref, order_ref, *refs):
+    sources, outs = refs[:-pieces - 4], refs[-pieces - 4:-4]
     total, x_ref, a_ref, sems = refs[-4:]
     *x_sources, a_source = sources[:x_ref.shape[0] // SLICE + 1]
     rows = total.shape[0] - 1
@@ -72,17 +73,17 @@
                 out[place * per + i] = total[start + i].astype(jnp.bfloat16)
 
 
-def partial_pieces(place, count, order, xs, tiles, rows, *before):
+def partial_pieces(place, count, order, xs, tiles, rows, parts, *before):
     feat, side = sum(x.shape[0] for x in xs), tiles.shape[-1]
     smem = pl.BlockSpec(memory_space=pltpu.SMEM)
     vmem = pl.BlockSpec(memory_space=pltpu.VMEM)
     hbm = pl.BlockSpec(memory_space=pltpu.HBM)
     piece = lambda part: jax.ShapeDtypeStruct((rows // part, feat, side), jnp.bfloat16)
     return pl.pallas_call(
-        tile_kernel,
-        out_shape=[piece(4), piece(4), piece(8), piece(8), piece(4)],
+        functools.partial(tile_kernel, len(parts)),
+        out_shape=[piece(part) for part in parts],
         in_specs=[smem, smem, smem] + [hbm] * (len(xs) + 1) + [pl.BlockSpec(memory_space=pl.ANY)] * len(before),
-        out_specs=[vmem] * PIECES,
+        out_specs=[vmem] * len(parts),
         scratch_shapes=[
             pltpu.VMEM((rows + 1, feat, side), jnp.float32),
             pltpu.VMEM((feat, xs[0].shape[1]), jnp.bfloat16),
@@ -114,26 +115,110 @@
 
 
 def start_y(pieces):
-    return send(pieces[2], along_y(1)), send(pieces[3], along_y(-1))
+    return send(pieces[4], along_y(1)), send(pieces[5], along_y(-1))
+
+
+def plain_y(pieces):
+    return send(pieces[3], along_y(1)), send(pieces[6], along_y(-1))
+
+
+def relay_kernel(*refs):
+    for near, far, out in zip(refs[:2], refs[2:4], refs[4:]):
+        out[...] = (near[...].astype(jnp.float32) + far[...].astype(jnp.float32)).astype(jnp.bfloat16)
 
 
 def relay_y(pieces, far):
-    next_up, next_down = pieces[1], pieces[4]
-    half = pieces[2].shape[0]
-    up = jnp.concatenate([add(next_up[:half], far[0]), next_up[half:]])
-    down = jnp.concatenate([next_down[:half], add(next_down[half:], far[1])])
-    return up, down
-
-
-def end_y(pieces, up, down):
-    near_up, near_down = send(up, along_y(1)), send(down, along_y(-1))
-    own = pieces[0]
-    n = own.shape[0] // Z
-    return [add(*(t[d * n:(d + 1) * n] for t in (own, near_up, near_down))) for d in range(Z)]
+    vmem = pl.BlockSpec(memory_space=pltpu.VMEM)
+    out = jax.ShapeDtypeStruct(far[0].shape, far[0].dtype)
+    return pl.pallas_call(
+        relay_kernel,
+        out_shape=[out, out],
+        in_specs=[vmem] * 4,
+        out_specs=[vmem] * 2,
+        compiler_params=pltpu.CompilerParams(vmem_limit_bytes=8 * 2**20),
+        name="relay_y",
+    )(pieces[2], pieces[7], *far)
+
+
+def relay_z(up, down, far_up, far_down):
+    block = lambda index: pl.BlockSpec(far_up.shape, lambda i: (index, 0, 0))
+    return pl.pallas_call(
+        relay_kernel,
+        grid=(1,),
+        out_shape=[jax.ShapeDtypeStruct(up.shape, up.dtype)] * 2,
+        in_specs=[block(0), block(1), block(0), block(0)],
+        out_specs=[block(0), block(1)],
+        input_output_aliases={0: 0, 1: 1},
+        compiler_params=pltpu.CompilerParams(vmem_limit_bytes=8 * 2**20),
+        name="relay_z",
+    )(up, down, far_up, far_down)
+
+
+def sum_kernel(wholes, *refs):
+    whole, halved, outs = refs[:wholes], refs[wholes:-5], refs[-5:]
+    mine_ref, up_ref, far_up_ref, far_down_ref, down_ref = outs
+    n = mine_ref.shape[0]
+
+    def total(refs, tile):
+        out = refs[0][tile].astype(jnp.float32)
+        for ref in refs[1:]:
+            out = out + ref[tile].astype(jnp.float32)
+        return out.astype(jnp.bfloat16)
+
+    def put(out_ref, tile, d, i):
+        few = whole[0].shape[1]
+        out_ref[tile, :few] = total(whole, d * n + i)
+        if halved:
+            out_ref[tile, few:] = total(halved[:3] if d < 2 else halved[3:], (d % 2) * n + i)
+
+    for i in range(n):
+        put(mine_ref, i, 0, i)
+        put(up_ref, i, 1, i)
+        put(far_up_ref if i < n // 2 else far_down_ref, i % (n // 2), 2, i)
+        put(down_ref, i, 3, i)
+
+
+def sum_y(whole, first=(), last=()):
+    n = whole[0].shape[0] // Z
+    feat = sum(terms[0].shape[1] for terms in (whole, first) if terms)
+    out = lambda count: jax.ShapeDtypeStruct((count, feat, whole[0].shape[2]), jnp.bfloat16)
+    vmem = pl.BlockSpec(memory_space=pltpu.VMEM)
+    terms = [*whole, *first, *last]
+    return pl.pallas_call(
+        functools.partial(sum_kernel, len(whole)),
+        out_shape=[out(n), out(n), out(n // 2), out(n // 2), out(n)],
+        in_specs=[vmem] * len(terms),
+        out_specs=[vmem] * 5,
+        compiler_params=pltpu.CompilerParams(vmem_limit_bytes=16 * 2**20),
+        name="sum_y",
+    )(*terms)
+
+
+def relays_z(mine, up, far_up, far_down, down):
+    far_up, far_down = send(far_up, along_z(1)), send(far_down, along_z(-1))
+    return relay_z(up, down, far_up, far_down)
+
+
+def end_z(mine, relayed):
+    return add(mine, send(relayed[0], along_z(1)), send(relayed[1], along_z(-1)))
+
+
+def ends_y(pieces, plain, relayed):
+    up, down = send(relayed[0], along_y(1)), send(relayed[1], along_y(-1))
+    return [pieces[0], up, plain[1]], [pieces[1], plain[0], down]
+
+
+def parts_of(count, *terms):
+    n = terms[0].shape[0] // count
+    return [add(*(t[d * n:(d + 1) * n] for t in terms)) for d in range(count)]
 
 
 def sum_z(mine):
     return add(mine[0], *(send(mine[d], along_z(d)) for d in (1, 2, 3)))
+
+
+def all_y(pieces):
+    return send(pieces[1], along_y(1)), send(pieces[3], along_y(-1)), send(pieces[2], along_y(2))
 
 
 def row_step(along_x, other_z, other_core):
@@ -158,7 +243,7 @@
         for dy, dzs in ((0, range(4)), (1, range(4)), (2, (0, 1)), (2, (2, 3)), (3, range(4)))
         for dz in dzs
     ])
-    kernel = lambda xs, *before: partial_pieces(place, count, order, xs, tiles, rows, *before)
+    kernel = lambda parts, xs, *before: partial_pieces(place, count, order, xs, tiles, rows, parts, *before)
     own = features.T
     weights = weight.reshape(lax.axis_size("row"), own.shape[0], -1)
     r = lax.axis_index("row")
@@ -174,31 +259,29 @@
     side = [get(own, 1, 0, 0), get(own, -1, 0, 0)]
     near = [own, pair]
     near += swap(near)
-    pieces_a = kernel(near, *side)
-    side += [get(pair, 1, 0, 0), get(pair, -1, 0, 0)]
-    far_a = start_y(pieces_a)
-    side = then(pieces_a, side)
+    pieces_a = kernel(WHOLE, near, *side)
+    pair_side = [get(pair, 1, 0, 0), get(pair, -1, 0, 0)]
     swapped = swap(side)
-    relay_a = relay_y(pieces_a, far_a)
-    pieces_b = kernel(side + swapped, *relay_a)
-    side = then(swapped, side)
-    far = [get(side[0], 1, 0, 0), get(side[3], -1, 0, 0)]
-    mine_a = end_y(pieces_a, *relay_a)
+    near_a = all_y(then(swapped, pieces_a))
+    pair_side = then(pieces_a, pair_side)
+    swapped += swap(pair_side)
+    side, pair_side = then(swapped, (side, pair_side))
+    far = [get(side[0], 1, 0, 0), get(pair_side[1], -1, 0, 0)]
+    pieces_b = kernel(HALVED, side + pair_side + swapped)
     far_b = start_y(pieces_b)
-    far = then(pieces_b, far)
-    pieces_c = kernel(far + swap(far), *mine_a)
-    hidden_a = sum_z(mine_a)
-    far_c = start_y(pieces_c)
+    far = then((pieces_b, near_a), far)
+    far_swapped = swap(far)
+    plain_b = plain_y(then(far_swapped, pieces_b))
     relay_b = relay_y(pieces_b, far_b)
-    mine_b = end_y(pieces_b, *relay_b)
-    relay_c = relay_y(pieces_c, then(hidden_a, far_c))
-    mine_c = end_y(pieces_c, *relay_c)
-    hidden_b = sum_z(mine_b)
-    hidden_c = sum_z(mine_c)
+    pieces_c = kernel(WHOLE, far + far_swapped, *relay_b)
+    near_c = all_y(pieces_c)
+    mine = sum_y([pieces_a[0], *near_a], *ends_y(pieces_b, plain_b, relay_b))
+    relayed = relays_z(*mine)
+    hidden = end_z(mine[0], relayed)
+    hidden_c = sum_z(parts_of(Z, pieces_c[0], *then(relayed, near_c)))
     on = lambda chunk: [(dx, dz, core) for core in range(2) for dx, dz in chunk]
-    mixed = bias_vector + product(hidden_a, on([(0, 0), (0, 1)]))
-    mixed = mixed + product(hidden_b, on([(-1, 0), (1, 0), (-1, 1), (1, 1)]))
-    mixed = mixed + product(hidden_c, on([(2, 0), (2, 1)]))
+    near = on([(0, 0), (0, 1)]) + on([(-1, 0), (1, 0), (-1, 1), (1, 1)])
+    mixed = bias_vector + product(hidden, near) + product(hidden_c, on([(2, 0), (2, 1)]))
     embedded = jnp.maximum(mixed, jnp.float32(0.0)).astype(jnp.bfloat16)
     return embedded.reshape(-1, embedded.shape[-1])
 

time: 174 us -> 156 us (0.90)
  the two profiles are of different devices: /device:TPU:64 before, /device:TPU:34 now
where the time goes in v2:
time: 156 us
  waiting for transfers between devices  61.5 us (39%)
  starting transfers between devices  53 us (34%)
  Pallas kernels  18.8 us (12%)
  local copies, waits for them, and re-layouts  16.3 us (10%)
  matrix products  3.6 us (2%)
  other arithmetic  1.69 us (1%)
    ppermute x19, waiting for transfers between devices, send(): return lax.ppermute(v, 'col', perm)  45.9 us
    ppermute x19, starting transfers between devices, send(): return lax.ppermute(v, 'col', perm)  44.9 us
    ppermute x15, waiting for transfers between devices, shards(): get = lambda v, *step: lax.ppermute(v, 'row', row_step(*step))  15.6 us
    unnamed x54, local copies, waits for them, and re-layouts  15 us
    pallas_call x3, Pallas kernels, partial_pieces(): pl.pallas_call(functools.partial(tile_kernel, len(parts)), out_shape=[pie...  14.2 us
    ppermute x15, starting transfers between devices, shards(): get = lambda v, *step: lax.ppermute(v, 'row', row_step(*step))  8.12 us
    dot_general x2, matrix products, product(): jnp.einsum('tfm,fg->tmg', hidden, w, preferred_element_type=jnp.float32)  3.6 us
  transfers between devices with their start and end apart: 34, of which 11 were waited for; matrix products, arithmetic and copies ran while one was open for 3% of the time, Pallas kernels for 12%

profile of v2, /device:TPU:34, one launch (start us, length us, event | category | flops | bytes accessed | tf_op | source)
XLA Modules:
  0.0 155.8 jit_solution(14566952035738753742)
XLA Ops:
  0.1 1.6 %collective-permute-start.3 = (bf16[16,16384]{1,0:T(8,128)(2,1)}, bf16[16,16384]{1,0:T(8,128)(2,1)S(1)}, u32[]{:S(2)}, u32[]{:S(2)}) collective-permute-start(bf16[16,16384]{1,0:T(8,128)(2,1)} %bitcast.59), channel_id=1, source_target_pairs={{0,64},{16,80},{32,96},{48,112},{64,128},{80,144},{96,160},{112,17... | collective-permute-start | bytes 1572872 | tf_op jit(solution)/shard_map/ppermute | solution.py:256
  1.7 0.7 collective-permute-start.4
  2.4 11.6 %collective-permute-done.refs_1_ = bf16[16,16384]{1,0:T(8,128)(2,1)} collective-permute-done((bf16[16,16384]{1,0:T(8,128)(2,1)}, bf16[16,16384]{1,0:T(8,128)(2,1)}, u32[]{:S(2)}, u32[]{:S(2)}) %collective-permute-start) | collective-permute-done | bytes 524320 | tf_op jit(solution)/shard_map/ppermute | solution.py:256
  14.0 1.5 collective-permute-start.10
  15.5 0.8 copy-done.12
  16.3 0.5 collective-permute-start.11
  18.1 0.8 copy-done.14
  18.9 1.0 copy-done.1
  19.9 1.0 copy-done.13
  21.0 1.0 copy-done.15
  22.0 0.7 copy-done.23
  22.7 3.9 %tile_sum.3 = (bf16[32,64,128]{2,1,0:T(8,128)(2,1)S(1)}, bf16[32,64,128]{2,1,0:T(8,128)(2,1)S(1)}, bf16[32,64,128]{2,1,0:T(8,128)(2,1)S(1)}, bf16[32,64,128]{2,1,0:T(8,128)(2,1)S(1)}) custom-call(s32[2,192]{1,0:T(2,128)S(1)} %bitcast.62, s32[1]{0:T(128)} %bitcast.52.count_ref, s32[16]{0:T(128)S(1)} %stack.121.order_ref, bf16[16,16384]{1,0:T(8,128)(2,1)S(1)} %bitcast.61, ...), custom_call_target="tpu_custom_call" | custom-call | tf_op jit(solution)/shard_map/tile_sum/pallas_call | solution.py:82
  26.6 1.9 %collective-permute-done.10.refs_2_ = bf16[16,16384]{1,0:T(8,128)(2,1)S(1)} collective-permute-done((bf16[16,16384]{1,0:T(8,128)(2,1)}, bf16[16,16384]{1,0:T(8,128)(2,1)S(1)}, u32[]{:S(2)}, u32[]{:S(2)}) %collective-permute-start.10) | collective-permute-done | bytes 524320 | tf_op jit(solution)/shard_map/ppermute | solution.py:256
  28.5 2.0 %collective-permute-done.11.refs_3_ = bf16[16,16384]{1,0:T(8,128)(2,1)S(1)} collective-permute-done((bf16[16,16384]{1,0:T(8,128)(2,1)}, bf16[16,16384]{1,0:T(8,128)(2,1)S(1)}, u32[]{:S(2)}, u32[]{:S(2)}) %collective-permute-start.11) | collective-permute-done | bytes 524320 | tf_op jit(solution)/shard_map/ppermute | solution.py:256
  30.5 0.5 collective-permute-start.13
  31.1 0.8 copy-done.4
  31.9 1.6 %collective-permute-start.7 = (bf16[32,64,128]{2,1,0:T(8,128)(2,1)S(1)}, bf16[32,64,128]{2,1,0:T(8,128)(2,1)S(1)}, u32[]{:S(2)}, u32[]{:S(2)}) collective-permute-start(bf16[32,64,128]{2,1,0:T(8,128)(2,1)S(1)} %get-tuple-element.50), channel_id=1, source_target_pairs={{0,4},{1,5},{2,6},{3,7},{4,8},{5,9},{6,10},{7,11},{8,12},{9,13},{1... | collective-permute-start | bytes 1572872 | tf_op jit(solution)/shard_map/ppermute | solution.py:114
  33.4 1.7 %collective-permute-start.8 = (bf16[32,64,128]{2,1,0:T(8,128)(2,1)S(1)}, bf16[32,64,128]{2,1,0:T(8,128)(2,1)S(1)}, u32[]{:S(2)}, u32[]{:S(2)}) collective-permute-start(bf16[32,64,128]{2,1,0:T(8,128)(2,1)S(1)} %get-tuple-element.51), channel_id=1, source_target_pairs={{0,12},{1,13},{2,14},{3,15},{4,0},{5,1},{6,2},{7,3},{8,4},{9,5},{1... | collective-permute-start | bytes 1572872 | tf_op jit(solution)/shard_map/ppermute | solution.py:114
  35.1 2.0 %collective-permute-start.9 = (bf16[32,64,128]{2,1,0:T(8,128)(2,1)S(1)}, bf16[32,64,128]{2,1,0:T(8,128)(2,1)S(1)}, u32[]{:S(2)}, u32[]{:S(2)}) collective-permute-start(bf16[32,64,128]{2,1,0:T(8,128)(2,1)S(1)} %get-tuple-element.52), channel_id=1, source_target_pairs={{0,8},{1,9},{2,10},{3,11},{4,12},{5,13},{6,14},{7,15},{8,0},{9,1},... | collective-permute-start | bytes 1572872 | tf_op jit(solution)/shard_map/ppermute | solution.py:114
  37.1 1.3 collective-permute-start.17
  38.4 0.8 collective-permute-start.18
  39.2 1.0 copy-done.5
  40.2 5.4 %tile_sum.4 = (bf16[16,128,128]{2,1,0:T(8,128)(2,1)S(1)}, bf16[16,128,128]{2,1,0:T(8,128)(2,1)S(1)}, bf16[16,128,128]{2,1,0:T(8,128)(2,1)S(1)}, bf16[16,128,128]...) custom-call(s32[2,192]{1,0:T(2,128)S(1)} %bitcast.63, ...), custom_call_target="tpu_custom_call" | custom-call | tf_op jit(solution)/shard_map/tile_sum/pallas_call | solution.py:82
  45.7 0.8 copy-done.8
  46.5 0.8 copy-done.10
  47.3 2.5 %collective-permute-start.14 = (bf16[16,128,128]{2,1,0:T(8,128)(2,1)S(1)}, bf16[16,128,128]{2,1,0:T(8,128)(2,1)S(1)}, u32[]{:S(2)}, u32[]{:S(2)}) collective-permute-start(bf16[16,128,128]{2,1,0:T(8,128)(2,1)S(1)} %get-tuple-element.62), channel_id=1, source_target_pairs={{0,4},{1,5},{2,6},{3,7},{4,8},{5,9},{6,10},{7,11},{8,12},{9,13},{1... | collective-permute-start | bytes 1572872 | tf_op jit(solution)/shard_map/ppermute | solution.py:114
  49.8 0.8 copy-done.2
  50.6 10.5 %collective-permute-start.15 = (bf16[16,128,128]{2,1,0:T(8,128)(2,1)S(1)}, bf16[16,128,128]{2,1,0:T(8,128)(2,1)S(1)}, u32[]{:S(2)}, u32[]{:S(2)}) collective-permute-start(bf16[16,128,128]{2,1,0:T(8,128)(2,1)S(1)} %get-tuple-element.63), channel_id=1, source_target_pairs={{0,12},{1,13},{2,14},{3,15},{4,0},{5,1},{6,2},{7,3},{8,4},{9,5},{1... | collective-permute-start | bytes 1572872 | tf_op jit(solution)/shard_map/ppermute | solution.py:114
  61.1 0.8 copy-done.6
  62.5 8.1 %collective-permute-done.14.refs_2_ = bf16[16,128,128]{2,1,0:T(8,128)(2,1)S(1)} collective-permute-done((bf16[16,128,128]{2,1,0:T(8,128)(2,1)S(1)}, bf16[16,128,128]{2,1,0:T(8,128)(2,1)S(1)}, u32[]{:S(2)}, u32[]{:S(2)}) %collective-permute-start.14) | collective-permute-done | bytes 524320 | tf_op jit(solution)/shard_map/ppermute | solution.py:114
  70.9 1.2 collective-permute-start.16
  72.1 2.1 %collective-permute-start.23 = (bf16[16,128,128]{2,1,0:T(8,128)(2,1)S(1)}, bf16[16,128,128]{2,1,0:T(8,128)(2,1)S(1)}, u32[]{:S(2)}, u32[]{:S(2)}) collective-permute-start(bf16[16,128,128]{2,1,0:T(8,128)(2,1)S(1)} %get-tuple-element.72.refs_6_), channel_id=1, source_target_pairs={{0,12},{1,13},{2,14},{3,15},{4,0},{5,1},{6,2},{7,3},{8,4},{9,5},{1... | collective-permute-start | bytes 1572872 | tf_op jit(solution)/shard_map/ppermute | solution.py:114
  74.2 0.6 collective-permute-start.21
  74.7 1.5 collective-permute-start.22
  76.2 4.9 %tile_sum.5 = (bf16[32,64,128]{2,1,0:T(8,128)(2,1)S(1)}, bf16[32,64,128]{2,1,0:T(8,128)(2,1)}, bf16[32,64,128]{2,1,0:T(8,128)(2,1)}, bf16[32,64,128]{2,1,0:T(8,128)(2,1)}) custom-call(s32[2,192]{1,0:T(2,128)S(1)} %bitcast.64, s32[1]{0:T(128)} %bitcast.54.count_ref, s32[16]{0:T(128)S(1)} %stack.121.order_ref, ...), custom_call_target="tpu_custom_call" | custom-call | tf_op jit(solution)/shard_map/tile_sum/pallas_call | solution.py:82
  81.2 0.8 copy-done.20
  81.9 1.5 collective-permute-start.28
  83.4 3.5 %collective-permute-done.16.refs_5_ = bf16[16,128,128]{2,1,0:T(8,128)(2,1)S(1)} collective-permute-done((bf16[16,128,128]{2,1,0:T(8,128)(2,1)S(1)}, bf16[16,128,128]{2,1,0:T(8,128)(2,1)S(1)}, u32[]{:S(2)}, u32[]{:S(2)}) %collective-permute-start.16) | collective-permute-done | bytes 524320 | tf_op jit(solution)/shard_map/ppermute | solution.py:114
  86.9 0.8 copy-done.16
  87.8 0.6 collective-permute-start.29
  88.4 0.8 copy-done.18
  89.3 1.4 collective-permute-start.30
  90.9 7.4 %collective-permute-done.21.refs_6_ = bf16[16,128,128]{2,1,0:T(8,128)(2,1)} collective-permute-done((bf16[16,128,128]{2,1,0:T(8,128)(2,1)}, bf16[16,128,128]{2,1,0:T(8,128)(2,1)}, u32[]{:S(2)}, u32[]{:S(2)}) %collective-permute-start.21) | collective-permute-done | bytes 524320 | tf_op jit(solution)/shard_map/ppermute | solution.py:114
  98.3 1.0 copy-done.17
  99.4 1.0 copy-done.19
  100.4 2.5 %sum_y.1 = (bf16[8,192,128]{2,1,0:T(8,128)(2,1)S(1)}, bf16[8,192,128]{2,1,0:T(8,128)(2,1)}, bf16[4,192,128]{2,1,0:T(8,128)(2,1)S(1)}, bf16[4,192,128]{2,1,0:T(8,128)(2,1)S(1)}, bf16[8,192,128]{2,1,0:T(8,128)(2,1)}) custom-call(bf16[32,64,128]{2,1,0:T(8,128)(2,1)S(1)} %get-tuple-element.46.refs_0_, bf16[32,64,128]{2,1,0:T(8,128)(2,1)S(1)} %collective-permute-done.7.refs_1_, ...), custom_call_target="tpu_custom_call" | custom-call | tf_op jit(solution)/shard_map/sum_y/pallas_call | solution.py:187
  102.9 3.3 %collective-permute-start.24 = (bf16[4,192,128]{2,1,0:T(8,128)(2,1)S(1)}, bf16[4,192,128]{2,1,0:T(8,128)(2,1)S(1)}, u32[]{:S(2)}, u32[]{:S(2)}) collective-permute-start(bf16[4,192,128]{2,1,0:T(8,128)(2,1)S(1)} %get-tuple-element.76), channel_id=1, source_target_pairs={{0,1},{1,2},{2,3},{3,0},{4,5},{5,6},{6,7},{7,4},{8,9},{9,10},{10,1... | collective-permute-start | bytes 589832 | tf_op jit(solution)/shard_map/ppermute | solution.py:114
  106.1 3.0 %collective-permute-start.25 = (bf16[4,192,128]{2,1,0:T(8,128)(2,1)S(1)}, bf16[4,192,128]{2,1,0:T(8,128)(2,1)S(1)}, u32[]{:S(2)}, u32[]{:S(2)}) collective-permute-start(bf16[4,192,128]{2,1,0:T(8,128)(2,1)S(1)} %get-tuple-element.77), channel_id=1, source_target_pairs={{0,3},{1,0},{2,1},{3,2},{4,7},{5,4},{6,5},{7,6},{8,11},{9,8},{10,9... | collective-permute-start | bytes 589832 | tf_op jit(solution)/shard_map/ppermute | solution.py:114
  109.1 6.8 %collective-permute-done.24.refs_2_ = bf16[4,192,128]{2,1,0:T(8,128)(2,1)S(1)} collective-permute-done((bf16[4,192,128]{2,1,0:T(8,128)(2,1)S(1)}, bf16[4,192,128]{2,1,0:T(8,128)(2,1)S(1)}, u32[]{:S(2)}, u32[]{:S(2)}) %collective-permute-start.24) | collective-permute-done | bytes 196640 | tf_op jit(solution)/shard_map/ppermute | solution.py:114
  115.9 1.3 collective-permute-done.25.refs_3_
  117.1 1.8 %relay_z.1 = (bf16[8,192,128]{2,1,0:T(8,128)(2,1)}, bf16[8,192,128]{2,1,0:T(8,128)(2,1)}) custom-call(bf16[8,192,128]{2,1,0:T(8,128)(2,1)} %get-tuple-element.74.refs_0_, bf16[8,192,128]{2,1,0:T(8,128)(2,1)} %get-tuple-element.75.refs_1_, bf16[4,192,128]{2,1,0:T(8,128)(2,1)S(1)} %collective-permute-done.24.refs_2_, ...), custom_call_target="tpu_custom_call", output_to_operand_aliasing={{0}: (0, {}), {1}: (1, {})} | custom-call | tf_op jit(solution)/shard_map/relay_z/pallas_call | solution.py:145
  119.0 1.4 collective-permute-start.27
  120.4 1.8 %collective-permute-start.26 = (bf16[8,192,128]{2,1,0:T(8,128)(2,1)}, bf16[8,192,128]{2,1,0:T(8,128)(2,1)S(1)}, u32[]{:S(2)}, u32[]{:S(2)}) collective-permute-start(bf16[8,192,128]{2,1,0:T(8,128)(2,1)} %get-tuple-element.78), channel_id=1, source_target_pairs={{0,1},{1,2},{2,3},{3,0},{4,5},{5,6},{6,7},{7,4},{8,9},{9,10},{10,1... | collective-permute-start | bytes 1179656 | tf_op jit(solution)/shard_map/ppermute | solution.py:114
  122.2 1.6 %add_convert_fusion.5 = (bf16[8,64,128]{2,1,0:T(8,128)(2,1)S(1)}, bf16[8,64,128]{2,1,0:T(8,128)(2,1)S(1)}, bf16[8,64,128]{2,1,0:T(8,128)(2,1)S(1)}) fusion(bf16[32,64,128]{2,1,0:T(8,128)(2,1)} %collective-permute-done.30, bf16[32,64,128]{2,1,0:T(8,128)(2,1)} %collective-permute-done.29, bf16[32,64,128]{2,1,0:T(8,128)(2,1)} %collective-permute-done.28, ...), kind=kLoop, calls=%fused_computation.10 | loop fusion | flops 1572864 | bytes 1966080 | tf_op jit(solution)/shard_map/convert_element_type | solution.py:110
  123.8 4.7 %collective-permute-start.33 = (bf16[8,64,128]{2,1,0:T(8,128)(2,1)S(1)}, bf16[8,64,128]{2,1,0:T(8,128)(2,1)S(1)}, u32[]{:S(2)}, u32[]{:S(2)}) collective-permute-start(bf16[8,64,128]{2,1,0:T(8,128)(2,1)S(1)} %get-tuple-element.88), channel_id=1, source_target_pairs={{0,3},{1,0},{2,1},{3,2},{4,7},{5,4},{6,5},{7,6},{8,11},{9,8},{10,9... | collective-permute-start | bytes 393224 | tf_op jit(solution)/shard_map/ppermute | solution.py:114
  128.4 3.1 %collective-permute-start.32 = (bf16[8,64,128]{2,1,0:T(8,128)(2,1)S(1)}, bf16[8,64,128]{2,1,0:T(8,128)(2,1)S(1)}, u32[]{:S(2)}, u32[]{:S(2)}) collective-permute-start(bf16[8,64,128]{2,1,0:T(8,128)(2,1)S(1)} %get-tuple-element.89), channel_id=1, source_target_pairs={{0,2},{1,3},{2,0},{3,1},{4,6},{5,7},{6,4},{7,5},{8,10},{9,11},{10,... | collective-permute-start | bytes 393224 | tf_op jit(solution)/shard_map/ppermute | solution.py:114
  131.5 0.6 collective-permute-start.31
  132.2 0.5 gather_fusion.1
  132.7 0.6 gather_fusion
  133.3 5.3 %collective-permute-done.33 = bf16[8,64,128]{2,1,0:T(8,128)(2,1)S(1)} collective-permute-done((bf16[8,64,128]{2,1,0:T(8,128)(2,1)S(1)}, bf16[8,64,128]{2,1,0:T(8,128)(2,1)S(1)}, u32[]{:S(2)}, u32[]{:S(2)}) %collective-permute-start.33) | collective-permute-done | bytes 131104 | tf_op jit(solution)/shard_map/ppermute | solution.py:114
  138.6 11.8 %collective-permute-done.32 = bf16[8,64,128]{2,1,0:T(8,128)(2,1)S(1)} collective-permute-done((bf16[8,64,128]{2,1,0:T(8,128)(2,1)S(1)}, bf16[8,64,128]{2,1,0:T(8,128)(2,1)S(1)}, u32[]{:S(2)}, u32[]{:S(2)}) %collective-permute-start.32) | collective-permute-done | bytes 131104 | tf_op jit(solution)/shard_map/ppermute | solution.py:114
  150.4 1.7 %collective-permute-done.31 = bf16[8,64,128]{2,1,0:T(8,128)(2,1)S(1)} collective-permute-done((bf16[8,64,128]{2,1,0:T(8,128)(2,1)S(1)}, bf16[8,64,128]{2,1,0:T(8,128)(2,1)S(1)}, u32[]{:S(2)}, u32[]{:S(2)}) %collective-permute-start.31) | collective-permute-done | bytes 131104 | tf_op jit(solution)/shard_map/ppermute | solution.py:114
  152.1 1.4 fusion.3
  153.6 2.1 %fusion.2 = bf16[8,128,256]{2,1,0:T(8,128)(2,1)} fusion(f32[8,128,256]{2,1,0:T(8,128)S(1)} %fusion.3, bf16[192,256,1]{1,0,2:T(8,128)(2,1)S(1)} %bitcast.68, f32[256]{0:T(256)S(1)} %copy-done.26, bf16[8,192,128]{2,1,0:T(8,128)(2,1)S(1)} %collective-permute-done.27, bf16[8,192,128]{2,1,0:T(8,128)(2,1)S(1)} %collective-permute-done.26, ...), kind=kOutput, calls=%fused_computation.5 | convolution fusion | flops 102891520 | bytes 2851840 | tf_op jit(solution)/shard_map/tfm,fg->tmg/dot_general | solution.py:254
  (75 shorter events, 1.9 us)
Async XLA Ops:
  0.0 132.2 %copy-start = (bf16[256,256]{1,0:T(8,128)(2,1)S(1)}, bf16[256,256]{1,0:T(8,128)(2,1)}, u32[]{:S(2)}) copy-start(bf16[256,256]{1,0:T(8,128)(2,1)} %param.10) | copy-start | bytes 393220
  0.0 39.2 %copy-start.24 = (s32[1,1,192,2]{2,3,1,0:T(2,128)S(1)}, s32[1,1,192,2]{2,3,1,0:T(2,128)}, u32[]{:S(2)}) copy-start(s32[1,1,192,2]{2,3,1,0:T(2,128)} %param.8) | copy-start | bytes 4612
  0.0 14.0 %collective-permute-start = (bf16[16,16384]{1,0:T(8,128)(2,1)}, bf16[16,16384]{1,0:T(8,128)(2,1)}, u32[]{:S(2)}, u32[]{:S(2)}) collective-permute-start(bf16[16,16384]{1,0:T(8,128)(2,1)} %bitcast.57), channel_id=1, source_target_pairs={{0,32},{16,48},{32,0},{48,16},{64,96},{80,112},{96,64},{112,80},{1... | collective-permute-start | bytes 1572872 | tf_op jit(solution)/shard_map/ppermute | solution.py:256
  0.1 15.4 %collective-permute-start.1 = (bf16[16,16384]{1,0:T(8,128)(2,1)}, bf16[16,16384]{1,0:T(8,128)(2,1)S(1)}, u32[]{:S(2)}, u32[]{:S(2)}) collective-permute-start(bf16[16,16384]{1,0:T(8,128)(2,1)} %bitcast.58), channel_id=1, source_target_pairs={{0,16},{16,0},{32,48},{48,32},{64,80},{80,64},{96,112},{112,96},{1... | collective-permute-start | bytes 1572872 | tf_op jit(solution)/shard_map/ppermute | solution.py:256
  0.1 16.7 %collective-permute-start.3 = (bf16[16,16384]{1,0:T(8,128)(2,1)}, bf16[16,16384]{1,0:T(8,128)(2,1)S(1)}, u32[]{:S(2)}, u32[]{:S(2)}) collective-permute-start(bf16[16,16384]{1,0:T(8,128)(2,1)} %bitcast.59), channel_id=1, source_target_pairs={{0,64},{16,80},{32,96},{48,112},{64,128},{80,144},{96,160},{112,17... | collective-permute-start | bytes 1572872 | tf_op jit(solution)/shard_map/ppermute | solution.py:256
  1.7 15.1 %collective-permute-start.4 = (bf16[16,16384]{1,0:T(8,128)(2,1)}, bf16[16,16384]{1,0:T(8,128)(2,1)S(1)}, u32[]{:S(2)}, u32[]{:S(2)}) collective-permute-start(bf16[16,16384]{1,0:T(8,128)(2,1)} %bitcast.60), channel_id=1, source_target_pairs={{0,192},{16,208},{32,224},{48,240},{64,0},{80,16},{96,32},{112,48}... | collective-permute-start | bytes 1572872 | tf_op jit(solution)/shard_map/ppermute | solution.py:256
  14.0 4.1 %collective-permute-start.2 = (bf16[16,16384]{1,0:T(8,128)(2,1)}, bf16[16,16384]{1,0:T(8,128)(2,1)S(1)}, u32[]{:S(2)}, u32[]{:S(2)}) collective-permute-start(bf16[16,16384]{1,0:T(8,128)(2,1)} %collective-permute-done.refs_1_), channel_id=1, source_target_pairs={{0,16},{16,0},{32,48},{48,32},{64,80},{80,64},{96,112},{112,96},{1... | collective-permute-start | bytes 1572872 | tf_op jit(solution)/shard_map/ppermute | solution.py:256
  14.0 14.5 %collective-permute-start.10 = (bf16[16,16384]{1,0:T(8,128)(2,1)}, bf16[16,16384]{1,0:T(8,128)(2,1)S(1)}, u32[]{:S(2)}, u32[]{:S(2)}) collective-permute-start(bf16[16,16384]{1,0:T(8,128)(2,1)} %collective-permute-done.refs_1_), channel_id=1, source_target_pairs={{0,64},{16,80},{32,96},{48,112},{64,128},{80,144},{96,160},{112,17... | collective-permute-start | bytes 1572872 | tf_op jit(solution)/shard_map/ppermute | solution.py:256
  15.5 0.8 copy-start.12
  16.3 14.3 %collective-permute-start.11 = (bf16[16,16384]{1,0:T(8,128)(2,1)}, bf16[16,16384]{1,0:T(8,128)(2,1)S(1)}, u32[]{:S(2)}, u32[]{:S(2)}) collective-permute-start(bf16[16,16384]{1,0:T(8,128)(2,1)} %collective-permute-done.refs_1_), channel_id=1, source_target_pairs={{0,192},{16,208},{32,224},{48,240},{64,0},{80,16},{96,32},{112,48}... | collective-permute-start | bytes 1572872 | tf_op jit(solution)/shard_map/ppermute | solution.py:256
  16.8 14.2 %collective-permute-start.5 = (bf16[16,16384]{1,0:T(8,128)(2,1)S(1)}, bf16[16,16384]{1,0:T(8,128)(2,1)S(1)}, u32[]{:S(2)}, u32[]{:S(2)}) collective-permute-start(bf16[16,16384]{1,0:T(8,128)(2,1)S(1)} %collective-permute-done.3.refs_5_.refs_0_), channel_id=1, source_target_pairs={{0,16},{16,0},{32,48},{48,32},{64,80},{80,64},{96,112},{112,96},{1... | collective-permute-start | bytes 1572872 | tf_op jit(solution)/shard_map/ppermute | solution.py:256
  16.8 15.0 %collective-permute-start.6 = (bf16[16,16384]{1,0:T(8,128)(2,1)S(1)}, bf16[16,16384]{1,0:T(8,128)(2,1)}, u32[]{:S(2)}, u32[]{:S(2)}) collective-permute-start(bf16[16,16384]{1,0:T(8,128)(2,1)S(1)} %collective-permute-done.4.refs_6_.refs_1_), channel_id=1, source_target_pairs={{0,16},{16,0},{32,48},{48,32},{64,80},{80,64},{96,112},{112,96},{1... | collective-permute-start | bytes 1572872 | tf_op jit(solution)/shard_map/ppermute | solution.py:256
  18.1 0.8 copy-start.14
  18.9 1.0 copy-start.1
  19.9 1.0 copy-start.13
  21.0 1.0 copy-start.15
  22.0 0.7 copy-start.23
  30.5 6.5 %collective-permute-start.12 = (bf16[16,16384]{1,0:T(8,128)(2,1)S(1)}, bf16[16,16384]{1,0:T(8,128)(2,1)S(1)}, u32[]{:S(2)}, u32[]{:S(2)}) collective-permute-start(bf16[16,16384]{1,0:T(8,128)(2,1)S(1)} %collective-permute-done.10.refs_2_), channel_id=1, source_target_pairs={{0,16},{16,0},{32,48},{48,32},{64,80},{80,64},{96,112},{112,96},{1... | collective-permute-start | bytes 1572872 | tf_op jit(solution)/shard_map/ppermute | solution.py:256
  30.5 6.5 %collective-permute-start.13 = (bf16[16,16384]{1,0:T(8,128)(2,1)S(1)}, bf16[16,16384]{1,0:T(8,128)(2,1)S(1)}, u32[]{:S(2)}, u32[]{:S(2)}) collective-permute-start(bf16[16,16384]{1,0:T(8,128)(2,1)S(1)} %collective-permute-done.11.refs_3_), channel_id=1, source_target_pairs={{0,16},{16,0},{32,48},{48,32},{64,80},{80,64},{96,112},{112,96},{1... | collective-permute-start | bytes 1572872 | tf_op jit(solution)/shard_map/ppermute | solution.py:256
  31.1 0.8 copy-start.4
  31.9 15.4 %collective-permute-start.7 = (bf16[32,64,128]{2,1,0:T(8,128)(2,1)S(1)}, bf16[32,64,128]{2,1,0:T(8,128)(2,1)S(1)}, u32[]{:S(2)}, u32[]{:S(2)}) collective-permute-start(bf16[32,64,128]{2,1,0:T(8,128)(2,1)S(1)} %get-tuple-element.50), channel_id=1, source_target_pairs={{0,4},{1,5},{2,6},{3,7},{4,8},{5,9},{6,10},{7,11},{8,12},{9,13},{1... | collective-permute-start | bytes 1572872 | tf_op jit(solution)/shard_map/ppermute | solution.py:114
  33.4 16.3 %collective-permute-start.8 = (bf16[32,64,128]{2,1,0:T(8,128)(2,1)S(1)}, bf16[32,64,128]{2,1,0:T(8,128)(2,1)S(1)}, u32[]{:S(2)}, u32[]{:S(2)}) collective-permute-start(bf16[32,64,128]{2,1,0:T(8,128)(2,1)S(1)} %get-tuple-element.51), channel_id=1, source_target_pairs={{0,12},{1,13},{2,14},{3,15},{4,0},{5,1},{6,2},{7,3},{8,4},{9,5},{1... | collective-permute-start | bytes 1572872 | tf_op jit(solution)/shard_map/ppermute | solution.py:114
  35.1 26.0 %collective-permute-start.9 = (bf16[32,64,128]{2,1,0:T(8,128)(2,1)S(1)}, bf16[32,64,128]{2,1,0:T(8,128)(2,1)S(1)}, u32[]{:S(2)}, u32[]{:S(2)}) collective-permute-start(bf16[32,64,128]{2,1,0:T(8,128)(2,1)S(1)} %get-tuple-element.52), channel_id=1, source_target_pairs={{0,8},{1,9},{2,10},{3,11},{4,12},{5,13},{6,14},{7,15},{8,0},{9,1},... | collective-permute-start | bytes 1572872 | tf_op jit(solution)/shard_map/ppermute | solution.py:114
  37.1 2.1 %copy-start.25 = (bf16[16,16384]{1,0:T(8,128)(2,1)}, bf16[16,16384]{1,0:T(8,128)(2,1)S(1)}, u32[]{:S(2)}) copy-start(bf16[16,16384]{1,0:T(8,128)(2,1)S(1)} %collective-permute-done.13.refs_7_) | copy-start | bytes 1572868
  37.1 24.8 %collective-permute-start.17 = (bf16[16,16384]{1,0:T(8,128)(2,1)S(1)}, bf16[16,16384]{1,0:T(8,128)(2,1)S(1)}, u32[]{:S(2)}, u32[]{:S(2)}) collective-permute-start(bf16[16,16384]{1,0:T(8,128)(2,1)S(1)} %collective-permute-done.3.refs_5_.refs_0_), channel_id=1, source_target_pairs={{0,64},{16,80},{32,96},{48,112},{64,128},{80,144},{96,160},{112,17... | collective-permute-start | bytes 1572872 | tf_op jit(solution)/shard_map/ppermute | solution.py:256
  38.4 23.5 %collective-permute-start.18 = (bf16[16,16384]{1,0:T(8,128)(2,1)S(1)}, bf16[16,16384]{1,0:T(8,128)(2,1)S(1)}, u32[]{:S(2)}, u32[]{:S(2)}) collective-permute-start(bf16[16,16384]{1,0:T(8,128)(2,1)S(1)} %collective-permute-done.11.refs_3_), channel_id=1, source_target_pairs={{0,192},{16,208},{32,224},{48,240},{64,0},{80,16},{96,32},{112,48}... | collective-permute-start | bytes 1572872 | tf_op jit(solution)/shard_map/ppermute | solution.py:256
  39.2 1.0 copy-start.5
  45.6 0.8 copy-start.8
  46.5 0.8 copy-start.10
  47.3 51.0 %copy-start.9 = (bf16[16,128,128]{2,1,0:T(8,128)(2,1)S(1)}, bf16[16,128,128]{2,1,0:T(8,128)(2,1)}, u32[]{:S(2)}) copy-start(bf16[16,128,128]{2,1,0:T(8,128)(2,1)} %copy-done.8) | copy-start | bytes 1572868
  47.3 23.4 %collective-permute-start.14 = (bf16[16,128,128]{2,1,0:T(8,128)(2,1)S(1)}, bf16[16,128,128]{2,1,0:T(8,128)(2,1)S(1)}, u32[]{:S(2)}, u32[]{:S(2)}) collective-permute-start(bf16[16,128,128]{2,1,0:T(8,128)(2,1)S(1)} %get-tuple-element.62), channel_id=1, source_target_pairs={{0,4},{1,5},{2,6},{3,7},{4,8},{5,9},{6,10},{7,11},{8,12},{9,13},{1... | collective-permute-start | bytes 1572872 | tf_op jit(solution)/shard_map/ppermute | solution.py:114
  49.8 0.8 copy-start.2
  50.6 47.7 %copy-start.3 = (bf16[32,64,128]{2,1,0:T(8,128)(2,1)S(1)}, bf16[32,64,128]{2,1,0:T(8,128)(2,1)}, u32[]{:S(2)}) copy-start(bf16[32,64,128]{2,1,0:T(8,128)(2,1)} %copy-done.2) | copy-start | bytes 1572868
  50.6 20.1 %collective-permute-start.15 = (bf16[16,128,128]{2,1,0:T(8,128)(2,1)S(1)}, bf16[16,128,128]{2,1,0:T(8,128)(2,1)S(1)}, u32[]{:S(2)}, u32[]{:S(2)}) collective-permute-start(bf16[16,128,128]{2,1,0:T(8,128)(2,1)S(1)} %get-tuple-element.63), channel_id=1, source_target_pairs={{0,12},{1,13},{2,14},{3,15},{4,0},{5,1},{6,2},{7,3},{8,4},{9,5},{1... | collective-permute-start | bytes 1572872 | tf_op jit(solution)/shard_map/ppermute | solution.py:114
  61.1 0.8 copy-start.6
  61.9 36.4 %copy-start.7 = (bf16[32,64,128]{2,1,0:T(8,128)(2,1)S(1)}, bf16[32,64,128]{2,1,0:T(8,128)(2,1)}, u32[]{:S(2)}) copy-start(bf16[32,64,128]{2,1,0:T(8,128)(2,1)} %copy-done.6) | copy-start | bytes 1572868
  61.9 36.4 %copy-start.11 = (bf16[16,128,128]{2,1,0:T(8,128)(2,1)S(1)}, bf16[16,128,128]{2,1,0:T(8,128)(2,1)}, u32[]{:S(2)}) copy-start(bf16[16,128,128]{2,1,0:T(8,128)(2,1)} %copy-done.10) | copy-start | bytes 1572868
  61.9 12.3 %collective-permute-start.19 = (bf16[16,16384]{1,0:T(8,128)(2,1)S(1)}, bf16[16,16384]{1,0:T(8,128)(2,1)S(1)}, u32[]{:S(2)}, u32[]{:S(2)}) collective-permute-start(bf16[16,16384]{1,0:T(8,128)(2,1)S(1)} %collective-permute-done.17.refs_0_), channel_id=1, source_target_pairs={{0,16},{16,0},{32,48},{48,32},{64,80},{80,64},{96,112},{112,96},{1... | collective-permute-start | bytes 1572872 | tf_op jit(solution)/shard_map/ppermute | solution.py:256
  62.0 12.2 %collective-permute-start.20 = (bf16[16,16384]{1,0:T(8,128)(2,1)S(1)}, bf16[16,16384]{1,0:T(8,128)(2,1)S(1)}, u32[]{:S(2)}, u32[]{:S(2)}) collective-permute-start(bf16[16,16384]{1,0:T(8,128)(2,1)S(1)} %collective-permute-done.18.refs_1_), channel_id=1, source_target_pairs={{0,16},{16,0},{32,48},{48,32},{64,80},{80,64},{96,112},{112,96},{1... | collective-permute-start | bytes 1572872 | tf_op jit(solution)/shard_map/ppermute | solution.py:256
  70.9 16.1 %collective-permute-start.16 = (bf16[16,128,128]{2,1,0:T(8,128)(2,1)S(1)}, bf16[16,128,128]{2,1,0:T(8,128)(2,1)S(1)}, u32[]{:S(2)}, u32[]{:S(2)}) collective-permute-start(bf16[16,128,128]{2,1,0:T(8,128)(2,1)S(1)} %get-tuple-element.64.refs_5_), channel_id=1, source_target_pairs={{0,4},{1,5},{2,6},{3,7},{4,8},{5,9},{6,10},{7,11},{8,12},{9,13},{1... | collective-permute-start | bytes 1572872 | tf_op jit(solution)/shard_map/ppermute | solution.py:114
  72.1 16.3 %collective-permute-start.23 = (bf16[16,128,128]{2,1,0:T(8,128)(2,1)S(1)}, bf16[16,128,128]{2,1,0:T(8,128)(2,1)S(1)}, u32[]{:S(2)}, u32[]{:S(2)}) collective-permute-start(bf16[16,128,128]{2,1,0:T(8,128)(2,1)S(1)} %get-tuple-element.72.refs_6_), channel_id=1, source_target_pairs={{0,12},{1,13},{2,14},{3,15},{4,0},{5,1},{6,2},{7,3},{8,4},{9,5},{1... | collective-permute-start | bytes 1572872 | tf_op jit(solution)/shard_map/ppermute | solution.py:114
  74.2 24.1 %collective-permute-start.21 = (bf16[16,128,128]{2,1,0:T(8,128)(2,1)}, bf16[16,128,128]{2,1,0:T(8,128)(2,1)}, u32[]{:S(2)}, u32[]{:S(2)}) collective-permute-start(bf16[16,128,128]{2,1,0:T(8,128)(2,1)} %get-tuple-element.70), channel_id=1, source_target_pairs={{0,12},{1,13},{2,14},{3,15},{4,0},{5,1},{6,2},{7,3},{8,4},{9,5},{1... | collective-permute-start | bytes 1572872 | tf_op jit(solution)/shard_map/ppermute | solution.py:114
  74.7 23.5 %collective-permute-start.22 = (bf16[16,128,128]{2,1,0:T(8,128)(2,1)}, bf16[16,128,128]{2,1,0:T(8,128)(2,1)}, u32[]{:S(2)}, u32[]{:S(2)}) collective-permute-start(bf16[16,128,128]{2,1,0:T(8,128)(2,1)} %get-tuple-element.71), channel_id=1, source_target_pairs={{0,4},{1,5},{2,6},{3,7},{4,8},{5,9},{6,10},{7,11},{8,12},{9,13},{1... | collective-permute-start | bytes 1572872 | tf_op jit(solution)/shard_map/ppermute | solution.py:114
  81.1 0.8 copy-start.20
  81.9 71.7 %copy-start.26 = (f32[256]{0:T(256)S(1)}, f32[256]{0:T(256)}, u32[]{:S(2)}) copy-start(f32[256]{0:T(256)} %param.11) | copy-start | bytes 3076
  81.9 40.2 %collective-permute-start.28 = (bf16[32,64,128]{2,1,0:T(8,128)(2,1)}, bf16[32,64,128]{2,1,0:T(8,128)(2,1)}, u32[]{:S(2)}, u32[]{:S(2)}) collective-permute-start(bf16[32,64,128]{2,1,0:T(8,128)(2,1)} %get-tuple-element.81), channel_id=1, source_target_pairs={{0,4},{1,5},{2,6},{3,7},{4,8},{5,9},{6,10},{7,11},{8,12},{9,13},{1... | collective-permute-start | bytes 1572872 | tf_op jit(solution)/shard_map/ppermute | solution.py:114
  86.9 0.8 copy-start.16
  87.8 34.4 %collective-permute-start.29 = (bf16[32,64,128]{2,1,0:T(8,128)(2,1)}, bf16[32,64,128]{2,1,0:T(8,128)(2,1)}, u32[]{:S(2)}, u32[]{:S(2)}) collective-permute-start(bf16[32,64,128]{2,1,0:T(8,128)(2,1)} %get-tuple-element.82), channel_id=1, source_target_pairs={{0,12},{1,13},{2,14},{3,15},{4,0},{5,1},{6,2},{7,3},{8,4},{9,5},{1... | collective-permute-start | bytes 1572872 | tf_op jit(solution)/shard_map/ppermute | solution.py:114
  88.4 0.8 copy-start.18
  89.3 32.9 %collective-permute-start.30 = (bf16[32,64,128]{2,1,0:T(8,128)(2,1)}, bf16[32,64,128]{2,1,0:T(8,128)(2,1)}, u32[]{:S(2)}, u32[]{:S(2)}) collective-permute-start(bf16[32,64,128]{2,1,0:T(8,128)(2,1)} %get-tuple-element.83), channel_id=1, source_target_pairs={{0,8},{1,9},{2,10},{3,11},{4,12},{5,13},{6,14},{7,15},{8,0},{9,1},... | collective-permute-start | bytes 1572872 | tf_op jit(solution)/shard_map/ppermute | solution.py:114
  98.3 1.0 copy-start.17
  99.3 1.0 copy-start.19
  100.4 21.8 %copy-start.21 = (bf16[32,64,128]{2,1,0:T(8,128)(2,1)S(1)}, bf16[32,64,128]{2,1,0:T(8,128)(2,1)}, u32[]{:S(2)}) copy-start(bf16[32,64,128]{2,1,0:T(8,128)(2,1)} %copy-done.20) | copy-start | bytes 1572868
  102.9 20.9 %copy-start.22 = (bf16[8,192,128]{2,1,0:T(8,128)(2,1)}, bf16[8,192,128]{2,1,0:T(8,128)(2,1)S(1)}, u32[]{:S(2)}) copy-start(bf16[8,192,128]{2,1,0:T(8,128)(2,1)S(1)} %get-tuple-element.73) | copy-start | bytes 1179652
  102.9 13.0 %collective-permute-start.24 = (bf16[4,192,128]{2,1,0:T(8,128)(2,1)S(1)}, bf16[4,192,128]{2,1,0:T(8,128)(2,1)S(1)}, u32[]{:S(2)}, u32[]{:S(2)}) collective-permute-start(bf16[4,192,128]{2,1,0:T(8,128)(2,1)S(1)} %get-tuple-element.76), channel_id=1, source_target_pairs={{0,1},{1,2},{2,3},{3,0},{4,5},{5,6},{6,7},{7,4},{8,9},{9,10},{10,1... | collective-permute-start | bytes 589832 | tf_op jit(solution)/shard_map/ppermute | solution.py:114
  106.1 11.0 %collective-permute-start.25 = (bf16[4,192,128]{2,1,0:T(8,128)(2,1)S(1)}, bf16[4,192,128]{2,1,0:T(8,128)(2,1)S(1)}, u32[]{:S(2)}, u32[]{:S(2)}) collective-permute-start(bf16[4,192,128]{2,1,0:T(8,128)(2,1)S(1)} %get-tuple-element.77), channel_id=1, source_target_pairs={{0,3},{1,0},{2,1},{3,2},{4,7},{5,4},{6,5},{7,6},{8,11},{9,8},{10,9... | collective-permute-start | bytes 589832 | tf_op jit(solution)/shard_map/ppermute | solution.py:114
  119.0 34.6 %collective-permute-start.27 = (bf16[8,192,128]{2,1,0:T(8,128)(2,1)}, bf16[8,192,128]{2,1,0:T(8,128)(2,1)S(1)}, u32[]{:S(2)}, u32[]{:S(2)}) collective-permute-start(bf16[8,192,128]{2,1,0:T(8,128)(2,1)} %get-tuple-element.79), channel_id=1, source_target_pairs={{0,3},{1,0},{2,1},{3,2},{4,7},{5,4},{6,5},{7,6},{8,11},{9,8},{10,9... | collective-permute-start | bytes 1179656 | tf_op jit(solution)/shard_map/ppermute | solution.py:114
  120.4 33.2 %collective-permute-start.26 = (bf16[8,192,128]{2,1,0:T(8,128)(2,1)}, bf16[8,192,128]{2,1,0:T(8,128)(2,1)S(1)}, u32[]{:S(2)}, u32[]{:S(2)}) collective-permute-start(bf16[8,192,128]{2,1,0:T(8,128)(2,1)} %get-tuple-element.78), channel_id=1, source_target_pairs={{0,1},{1,2},{2,3},{3,0},{4,5},{5,6},{6,7},{7,4},{8,9},{9,10},{10,1... | collective-permute-start | bytes 1179656 | tf_op jit(solution)/shard_map/ppermute | solution.py:114
  123.8 14.8 %collective-permute-start.33 = (bf16[8,64,128]{2,1,0:T(8,128)(2,1)S(1)}, bf16[8,64,128]{2,1,0:T(8,128)(2,1)S(1)}, u32[]{:S(2)}, u32[]{:S(2)}) collective-permute-start(bf16[8,64,128]{2,1,0:T(8,128)(2,1)S(1)} %get-tuple-element.88), channel_id=1, source_target_pairs={{0,3},{1,0},{2,1},{3,2},{4,7},{5,4},{6,5},{7,6},{8,11},{9,8},{10,9... | collective-permute-start | bytes 393224 | tf_op jit(solution)/shard_map/ppermute | solution.py:114
  128.4 22.0 %collective-permute-start.32 = (bf16[8,64,128]{2,1,0:T(8,128)(2,1)S(1)}, bf16[8,64,128]{2,1,0:T(8,128)(2,1)S(1)}, u32[]{:S(2)}, u32[]{:S(2)}) collective-permute-start(bf16[8,64,128]{2,1,0:T(8,128)(2,1)S(1)} %get-tuple-element.89), channel_id=1, source_target_pairs={{0,2},{1,3},{2,0},{3,1},{4,6},{5,7},{6,4},{7,5},{8,10},{9,11},{10,... | collective-permute-start | bytes 393224 | tf_op jit(solution)/shard_map/ppermute | solution.py:114
  131.5 20.6 %collective-permute-start.31 = (bf16[8,64,128]{2,1,0:T(8,128)(2,1)S(1)}, bf16[8,64,128]{2,1,0:T(8,128)(2,1)S(1)}, u32[]{:S(2)}, u32[]{:S(2)}) collective-permute-start(bf16[8,64,128]{2,1,0:T(8,128)(2,1)S(1)} %get-tuple-element.87), channel_id=1, source_target_pairs={{0,1},{1,2},{2,3},{3,0},{4,5},{5,6},{6,7},{7,4},{8,9},{9,10},{10,1... | collective-permute-start | bytes 393224 | tf_op jit(solution)/shard_map/ppermute | solution.py:114

commit v3 on v2

--- a/solution.py
+++ b/solution.py
@@ -11,7 +11,7 @@
 HALVED = (8,) * 8
 SLICE = 16
 LOTS = 4
-VMEM_LIMIT = 46 * 2**20
+VMEM_LIMIT = 44 * 2**20
 X, Y, Z = 4, 4, 4
 
 
@@ -214,7 +214,7 @@
 
 
 def sum_z(mine):
-    return add(mine[0], *(send(mine[d], along_z(d)) for d in (1, 2, 3)))
+    return [mine[0]] + [send(mine[d], along_z(d)) for d in (1, 2, 3)]
 
 
 def all_y(pieces):
@@ -281,7 +281,9 @@
     hidden_c = sum_z(parts_of(Z, pieces_c[0], *then(relayed, near_c)))
     on = lambda chunk: [(dx, dz, core) for core in range(2) for dx, dz in chunk]
     near = on([(0, 0), (0, 1)]) + on([(-1, 0), (1, 0), (-1, 1), (1, 1)])
-    mixed = bias_vector + product(hidden, near) + product(hidden_c, on([(2, 0), (2, 1)]))
+    mixed = bias_vector + product(hidden, near)
+    mixed, hidden_c = lax.optimization_barrier((mixed, hidden_c))
+    mixed = mixed + product(add(*hidden_c), on([(2, 0), (2, 1)]))
     embedded = jnp.maximum(mixed, jnp.float32(0.0)).astype(jnp.bfloat16)
     return embedded.reshape(-1, embedded.shape[-1])
 

time: 156 us -> 153 us (0.981)
  starting transfers between devices: 53 us -> 48.5 us
  matrix products: 3.6 us -> 1.7 us
  local copies, waits for them, and re-layouts: 16.3 us -> 18.1 us
    ppermute x19, starting transfers between devices: 44.9 us -> 40.4 us  [send(): return lax.ppermute(v, 'col', perm)]
    dot_general x2, matrix products: 3.6 us -> 1.7 us  [product(): jnp.einsum('tfm,fg->tmg', hidden, w, preferred_element_type=jnp.float32)]
    unnamed x54, local copies, waits for them, and re-layouts: 15 us -> 16.8 us
  transfers between devices with their start and end apart: 34 -> 34, of which waited for: 11 -> 11; matrix products, arithmetic and copies ran while one was open for 3% -> 3% of each run, Pallas kernels for 12% -> 13%
where the time goes in v3:
time: 153 us
  waiting for transfers between devices  60.8 us (40%)
  starting transfers between devices  48.5 us (32%)
  Pallas kernels  19.6 us (13%)
  local copies, waits for them, and re-layouts  18.1 us (12%)
  other arithmetic  3.02 us (2%)
  matrix products  1.7 us (1%)
    ppermute x19, waiting for transfers between devices, send(): return lax.ppermute(v, 'col', perm)  45.6 us
    ppermute x19, starting transfers between devices, send(): return lax.ppermute(v, 'col', perm)  40.4 us
    unnamed x54, local copies, waits for them, and re-layouts  16.8 us
    ppermute x15, waiting for transfers between devices, shards(): get = lambda v, *step: lax.ppermute(v, 'row', row_step(*step))  15.2 us
    pallas_call x3, Pallas kernels, partial_pieces(): pl.pallas_call(functools.partial(tile_kernel, len(parts)), out_shape=[pie...  13.9 us
    ppermute x15, starting transfers between devices, shards(): get = lambda v, *step: lax.ppermute(v, 'row', row_step(*step))  8.12 us
  transfers between devices with their start and end apart: 34, of which 11 were waited for; matrix products, arithmetic and copies ran while one was open for 3% of the time, Pallas kernels for 13%

profile of v3, /device:TPU:34, one launch (start us, length us, event | category | flops | bytes accessed | tf_op | source)
XLA Modules:
  0.0 152.7 jit_solution(9869258516390994058)
XLA Ops:
  0.1 1.6 %collective-permute-start.3 = (bf16[16,16384]{1,0:T(8,128)(2,1)}, bf16[16,16384]{1,0:T(8,128)(2,1)S(1)}, u32[]{:S(2)}, u32[]{:S(2)}) collective-permute-start(bf16[16,16384]{1,0:T(8,128)(2,1)} %bitcast.59), channel_id=1, source_target_pairs={{0,64},{16,80},{32,96},{48,112},{64,128},{80,144},{96,160},{112,17... | collective-permute-start | bytes 1572872 | tf_op jit(solution)/shard_map/ppermute | solution.py:256
  1.7 0.7 collective-permute-start.4
  2.4 11.5 %collective-permute-done.refs_1_ = bf16[16,16384]{1,0:T(8,128)(2,1)S(1)} collective-permute-done((bf16[16,16384]{1,0:T(8,128)(2,1)}, bf16[16,16384]{1,0:T(8,128)(2,1)S(1)}, u32[]{:S(2)}, u32[]{:S(2)}) %collective-permute-start) | collective-permute-done | bytes 524320 | tf_op jit(solution)/shard_map/ppermute | solution.py:256
  13.9 1.5 collective-permute-start.10
  15.4 0.8 copy-done.2
  18.1 0.8 copy-done.4
  18.9 1.0 copy-done.1
  19.9 1.0 copy-done.3
  21.0 1.0 copy-done.5
  22.0 0.7 copy-done.24
  22.7 3.8 %tile_sum.3 = (bf16[32,64,128]{2,1,0:T(8,128)(2,1)S(1)}, bf16[32,64,128]{2,1,0:T(8,128)(2,1)S(1)}, bf16[32,64,128]{2,1,0:T(8,128)(2,1)S(1)}, bf16[32,64,128]{2,1,0:T(8,128)(2,1)S(1)}) custom-call(s32[2,192]{1,0:T(2,128)S(1)} %bitcast.62, s32[1]{0:T(128)} %bitcast.52.count_ref, s32[16]{0:T(128)S(1)} %stack.121.order_ref, bf16[16,16384]{1,0:T(8,128)(2,1)S(1)} %bitcast.61, ...), custom_call_target="tpu_custom_call" | custom-call | tf_op jit(solution)/shard_map/tile_sum/pallas_call | solution.py:82
  26.5 1.7 %collective-permute-done.10.refs_2_ = bf16[16,16384]{1,0:T(8,128)(2,1)S(1)} collective-permute-done((bf16[16,16384]{1,0:T(8,128)(2,1)S(1)}, bf16[16,16384]{1,0:T(8,128)(2,1)S(1)}, u32[]{:S(2)}, u32[]{:S(2)}) %collective-permute-start.10) | collective-permute-done | bytes 524320 | tf_op jit(solution)/shard_map/ppermute | solution.py:256
  28.2 2.0 %collective-permute-done.11.refs_3_ = bf16[16,16384]{1,0:T(8,128)(2,1)S(1)} collective-permute-done((bf16[16,16384]{1,0:T(8,128)(2,1)S(1)}, bf16[16,16384]{1,0:T(8,128)(2,1)S(1)}, u32[]{:S(2)}, u32[]{:S(2)}) %collective-permute-start.11) | collective-permute-done | bytes 524320 | tf_op jit(solution)/shard_map/ppermute | solution.py:256
  30.7 1.6 %collective-permute-start.7 = (bf16[32,64,128]{2,1,0:T(8,128)(2,1)S(1)}, bf16[32,64,128]{2,1,0:T(8,128)(2,1)S(1)}, u32[]{:S(2)}, u32[]{:S(2)}) collective-permute-start(bf16[32,64,128]{2,1,0:T(8,128)(2,1)S(1)} %get-tuple-element.55), channel_id=1, source_target_pairs={{0,4},{1,5},{2,6},{3,7},{4,8},{5,9},{6,10},{7,11},{8,12},{9,13},{1... | collective-permute-start | bytes 1572872 | tf_op jit(solution)/shard_map/ppermute | solution.py:114
  32.3 1.7 %collective-permute-start.8 = (bf16[32,64,128]{2,1,0:T(8,128)(2,1)S(1)}, bf16[32,64,128]{2,1,0:T(8,128)(2,1)S(1)}, u32[]{:S(2)}, u32[]{:S(2)}) collective-permute-start(bf16[32,64,128]{2,1,0:T(8,128)(2,1)S(1)} %get-tuple-element.56), channel_id=1, source_target_pairs={{0,12},{1,13},{2,14},{3,15},{4,0},{5,1},{6,2},{7,3},{8,4},{9,5},{1... | collective-permute-start | bytes 1572872 | tf_op jit(solution)/shard_map/ppermute | solution.py:114
  34.0 2.0 %collective-permute-start.9 = (bf16[32,64,128]{2,1,0:T(8,128)(2,1)S(1)}, bf16[32,64,128]{2,1,0:T(8,128)(2,1)S(1)}, u32[]{:S(2)}, u32[]{:S(2)}) collective-permute-start(bf16[32,64,128]{2,1,0:T(8,128)(2,1)S(1)} %get-tuple-element.57), channel_id=1, source_target_pairs={{0,8},{1,9},{2,10},{3,11},{4,12},{5,13},{6,14},{7,15},{8,0},{9,1},... | collective-permute-start | bytes 1572872 | tf_op jit(solution)/shard_map/ppermute | solution.py:114
  36.0 1.2 collective-permute-start.17
  37.2 0.8 collective-permute-start.18
  38.0 5.2 %tile_sum.4 = (bf16[16,128,128]{2,1,0:T(8,128)(2,1)S(1)}, bf16[16,128,128]{2,1,0:T(8,128)(2,1)S(1)}, bf16[16,128,128]{2,1,0:T(8,128)(2,1)S(1)}, bf16[16,128,128]...) custom-call(s32[2,192]{1,0:T(2,128)S(1)} %bitcast.63, ...), custom_call_target="tpu_custom_call" | custom-call | tf_op jit(solution)/shard_map/tile_sum/pallas_call | solution.py:82
  43.2 0.8 copy-done.10
  44.0 0.8 copy-done.12
  44.8 1.1 collective-permute-done.7.refs_1_
  45.9 1.2 collective-permute-start.14
  47.1 8.4 %collective-permute-done.8.refs_2_ = bf16[32,64,128]{2,1,0:T(8,128)(2,1)S(1)} collective-permute-done((bf16[32,64,128]{2,1,0:T(8,128)(2,1)S(1)}, bf16[32,64,128]{2,1,0:T(8,128)(2,1)S(1)}, u32[]{:S(2)}, u32[]{:S(2)}) %collective-permute-start.8) | collective-permute-done | bytes 524320 | tf_op jit(solution)/shard_map/ppermute | solution.py:114
  55.5 0.8 copy-done.6
  56.3 4.2 %collective-permute-start.15 = (bf16[16,128,128]{2,1,0:T(8,128)(2,1)S(1)}, bf16[16,128,128]{2,1,0:T(8,128)(2,1)S(1)}, u32[]{:S(2)}, u32[]{:S(2)}) collective-permute-start(bf16[16,128,128]{2,1,0:T(8,128)(2,1)S(1)} %get-tuple-element.68), channel_id=1, source_target_pairs={{0,12},{1,13},{2,14},{3,15},{4,0},{5,1},{6,2},{7,3},{8,4},{9,5},{1... | collective-permute-start | bytes 1572872 | tf_op jit(solution)/shard_map/ppermute | solution.py:114
  60.5 0.8 copy-done.8
  61.4 0.8 copy-done.14
  62.7 0.8 copy-done.16
  63.5 6.1 %collective-permute-done.14.refs_2_ = bf16[16,128,128]{2,1,0:T(8,128)(2,1)S(1)} collective-permute-done((bf16[16,128,128]{2,1,0:T(8,128)(2,1)S(1)}, bf16[16,128,128]{2,1,0:T(8,128)(2,1)S(1)}, u32[]{:S(2)}, u32[]{:S(2)}) %collective-permute-start.14) | collective-permute-done | bytes 524320 | tf_op jit(solution)/shard_map/ppermute | solution.py:114
  69.6 1.2 relay_y.1
  70.7 1.1 collective-permute-start.16
  71.9 2.1 %collective-permute-start.23 = (bf16[16,128,128]{2,1,0:T(8,128)(2,1)}, bf16[16,128,128]{2,1,0:T(8,128)(2,1)}, u32[]{:S(2)}, u32[]{:S(2)}) collective-permute-start(bf16[16,128,128]{2,1,0:T(8,128)(2,1)} %get-tuple-element.77.refs_6_), channel_id=1, source_target_pairs={{0,12},{1,13},{2,14},{3,15},{4,0},{5,1},{6,2},{7,3},{8,4},{9,5},{1... | collective-permute-start | bytes 1572872 | tf_op jit(solution)/shard_map/ppermute | solution.py:114
  74.0 0.8 copy-done.18
  74.8 0.8 copy-done.20
  75.7 0.6 collective-permute-start.21
  76.3 1.4 collective-permute-start.22
  77.8 1.0 copy-done.15
  78.8 1.0 copy-done.17
  79.9 1.0 copy-done.19
  80.9 1.0 copy-done.21
  82.0 4.9 %tile_sum.5 = (bf16[32,64,128]{2,1,0:T(8,128)(2,1)S(1)}, bf16[32,64,128]{2,1,0:T(8,128)(2,1)}, bf16[32,64,128]{2,1,0:T(8,128)(2,1)}, bf16[32,64,128]{2,1,0:T(8,128)(2,1)}) custom-call(s32[2,192]{1,0:T(2,128)S(1)} %bitcast.64, s32[1]{0:T(128)} %bitcast.54.count_ref, s32[16]{0:T(128)S(1)} %stack.121.order_ref, bf16[16,16384]{1,0:T(8,128)(2,1)S(1)} %copy-done.15, ...), custom_call_target="tpu_custom_call" | custom-call | tf_op jit(solution)/shard_map/tile_sum/pallas_call | solution.py:82
  86.9 1.0 collective-permute-start.28
  87.9 2.4 %collective-permute-start.29 = (bf16[32,64,128]{2,1,0:T(8,128)(2,1)}, bf16[32,64,128]{2,1,0:T(8,128)(2,1)}, u32[]{:S(2)}, u32[]{:S(2)}) collective-permute-start(bf16[32,64,128]{2,1,0:T(8,128)(2,1)} %get-tuple-element.87), channel_id=1, source_target_pairs={{0,12},{1,13},{2,14},{3,15},{4,0},{5,1},{6,2},{7,3},{8,4},{9,5},{1... | collective-permute-start | bytes 1572872 | tf_op jit(solution)/shard_map/ppermute | solution.py:114
  90.2 1.4 collective-permute-start.30
  91.6 6.7 %collective-permute-done.21.refs_6_ = bf16[16,128,128]{2,1,0:T(8,128)(2,1)} collective-permute-done((bf16[16,128,128]{2,1,0:T(8,128)(2,1)}, bf16[16,128,128]{2,1,0:T(8,128)(2,1)}, u32[]{:S(2)}, u32[]{:S(2)}) %collective-permute-start.21) | collective-permute-done | bytes 524320 | tf_op jit(solution)/shard_map/ppermute | solution.py:114
  98.3 2.8 %sum_y.1 = (bf16[8,192,128]{2,1,0:T(8,128)(2,1)S(1)}, bf16[8,192,128]{2,1,0:T(8,128)(2,1)}, bf16[4,192,128]{2,1,0:T(8,128)(2,1)}, bf16[4,192,128]{2,1,0:T(8,128)(2,1)S(1)}, bf16[8,192,128]{2,1,0:T(8,128)(2,1)}) custom-call(bf16[32,64,128]{2,1,0:T(8,128)(2,1)S(1)} %get-tuple-element.51.refs_0_, bf16[32,64,128]{2,1,0:T(8,128)(2,1)S(1)} %collective-permute-done.7.refs_1_, ...), custom_call_target="tpu_custom_call" | custom-call | tf_op jit(solution)/shard_map/sum_y/pallas_call | solution.py:187
  101.1 0.8 copy-done.23
  101.9 3.3 %collective-permute-start.24 = (bf16[4,192,128]{2,1,0:T(8,128)(2,1)}, bf16[4,192,128]{2,1,0:T(8,128)(2,1)S(1)}, u32[]{:S(2)}, u32[]{:S(2)}) collective-permute-start(bf16[4,192,128]{2,1,0:T(8,128)(2,1)} %get-tuple-element.81), channel_id=1, source_target_pairs={{0,1},{1,2},{2,3},{3,0},{4,5},{5,6},{6,7},{7,4},{8,9},{9,10},{10,1... | collective-permute-start | bytes 589832 | tf_op jit(solution)/shard_map/ppermute | solution.py:114
  105.1 2.9 %collective-permute-start.25 = (bf16[4,192,128]{2,1,0:T(8,128)(2,1)S(1)}, bf16[4,192,128]{2,1,0:T(8,128)(2,1)S(1)}, u32[]{:S(2)}, u32[]{:S(2)}) collective-permute-start(bf16[4,192,128]{2,1,0:T(8,128)(2,1)S(1)} %get-tuple-element.82), channel_id=1, source_target_pairs={{0,3},{1,0},{2,1},{3,2},{4,7},{5,4},{6,5},{7,6},{8,11},{9,8},{10,9... | collective-permute-start | bytes 589832 | tf_op jit(solution)/shard_map/ppermute | solution.py:114
  108.1 7.2 %collective-permute-done.24.refs_2_ = bf16[4,192,128]{2,1,0:T(8,128)(2,1)S(1)} collective-permute-done((bf16[4,192,128]{2,1,0:T(8,128)(2,1)}, bf16[4,192,128]{2,1,0:T(8,128)(2,1)S(1)}, u32[]{:S(2)}, u32[]{:S(2)}) %collective-permute-start.24) | collective-permute-done | bytes 196640 | tf_op jit(solution)/shard_map/ppermute | solution.py:114
  115.2 1.8 %relay_z.1 = (bf16[8,192,128]{2,1,0:T(8,128)(2,1)}, bf16[8,192,128]{2,1,0:T(8,128)(2,1)}) custom-call(bf16[8,192,128]{2,1,0:T(8,128)(2,1)} %get-tuple-element.79.refs_0_, bf16[8,192,128]{2,1,0:T(8,128)(2,1)} %get-tuple-element.80.refs_1_, bf16[4,192,128]{2,1,0:T(8,128)(2,1)S(1)} %collective-permute-done.24.refs_2_, ...), custom_call_target="tpu_custom_call", output_to_operand_aliasing={{0}: (0, {}), {1}: (1, {})} | custom-call | tf_op jit(solution)/shard_map/relay_z/pallas_call | solution.py:145
  117.1 2.6 %collective-permute-start.27 = (bf16[8,192,128]{2,1,0:T(8,128)(2,1)}, bf16[8,192,128]{2,1,0:T(8,128)(2,1)S(1)}, u32[]{:S(2)}, u32[]{:S(2)}) collective-permute-start(bf16[8,192,128]{2,1,0:T(8,128)(2,1)} %get-tuple-element.84), channel_id=1, source_target_pairs={{0,3},{1,0},{2,1},{3,2},{4,7},{5,4},{6,5},{7,6},{8,11},{9,8},{10,9... | collective-permute-start | bytes 1179656 | tf_op jit(solution)/shard_map/ppermute | solution.py:114
  119.7 1.3 collective-permute-start.26
  121.1 0.6 gather_fusion
  122.3 2.0 %add_convert_fusion.3 = (bf16[8,64,128]{2,1,0:T(8,128)(2,1)S(1)}, bf16[8,64,128]{2,1,0:T(8,128)(2,1)S(1)}, bf16[8,64,128]{2,1,0:T(8,128)(2,1)S(1)}, bf16[8,64,128]{2,1,0:T(8,128)(2,1)S(1)}) fusion(bf16[32,64,128]{2,1,0:T(8,128)(2,1)} %collective-permute-done.30, bf16[32,64,128]{2,1,0:T(8,128)(2,1)} %collective-permute-done.29, ...), kind=kLoop, calls=%fused_computation.6 | loop fusion | flops 2097152 | bytes 2621440 | tf_op jit(solution)/shard_map/convert_element_type | solution.py:110
  124.3 4.2 %collective-permute-start.31 = (bf16[8,64,128]{2,1,0:T(8,128)(2,1)S(1)}, bf16[8,64,128]{2,1,0:T(8,128)(2,1)S(1)}, u32[]{:S(2)}, u32[]{:S(2)}) collective-permute-start(bf16[8,64,128]{2,1,0:T(8,128)(2,1)S(1)} %get-tuple-element.99), channel_id=1, source_target_pairs={{0,1},{1,2},{2,3},{3,0},{4,5},{5,6},{6,7},{7,4},{8,9},{9,10},{10,1... | collective-permute-start | bytes 393224 | tf_op jit(solution)/shard_map/ppermute | solution.py:114
  128.5 2.9 %collective-permute-start.32 = (bf16[8,64,128]{2,1,0:T(8,128)(2,1)S(1)}, bf16[8,64,128]{2,1,0:T(8,128)(2,1)S(1)}, u32[]{:S(2)}, u32[]{:S(2)}) collective-permute-start(bf16[8,64,128]{2,1,0:T(8,128)(2,1)S(1)} %get-tuple-element.98), channel_id=1, source_target_pairs={{0,2},{1,3},{2,0},{3,1},{4,6},{5,7},{6,4},{7,5},{8,10},{9,11},{10,... | collective-permute-start | bytes 393224 | tf_op jit(solution)/shard_map/ppermute | solution.py:114
  131.4 2.5 %collective-permute-start.33 = (bf16[8,64,128]{2,1,0:T(8,128)(2,1)S(1)}, bf16[8,64,128]{2,1,0:T(8,128)(2,1)S(1)}, u32[]{:S(2)}, u32[]{:S(2)}) collective-permute-start(bf16[8,64,128]{2,1,0:T(8,128)(2,1)S(1)} %get-tuple-element.97), channel_id=1, source_target_pairs={{0,3},{1,0},{2,1},{3,2},{4,7},{5,4},{6,5},{7,6},{8,11},{9,8},{10,9... | collective-permute-start | bytes 393224 | tf_op jit(solution)/shard_map/ppermute | solution.py:114
  133.9 3.1 %collective-permute-done.27 = bf16[8,192,128]{2,1,0:T(8,128)(2,1)S(1)} collective-permute-done((bf16[8,192,128]{2,1,0:T(8,128)(2,1)}, bf16[8,192,128]{2,1,0:T(8,128)(2,1)S(1)}, u32[]{:S(2)}, u32[]{:S(2)}) %collective-permute-start.27) | collective-permute-done | bytes 393248 | tf_op jit(solution)/shard_map/ppermute | solution.py:114
  137.1 2.4 %collective-permute-done.26 = bf16[8,192,128]{2,1,0:T(8,128)(2,1)S(1)} collective-permute-done((bf16[8,192,128]{2,1,0:T(8,128)(2,1)}, bf16[8,192,128]{2,1,0:T(8,128)(2,1)S(1)}, u32[]{:S(2)}, u32[]{:S(2)}) %collective-permute-start.26) | collective-permute-done | bytes 393248 | tf_op jit(solution)/shard_map/ppermute | solution.py:114
  139.5 1.3 convolution_add_fusion
  140.8 10.5 %collective-permute-done.31 = bf16[8,64,128]{2,1,0:T(8,128)(2,1)S(1)} collective-permute-done((bf16[8,64,128]{2,1,0:T(8,128)(2,1)S(1)}, bf16[8,64,128]{2,1,0:T(8,128)(2,1)S(1)}, u32[]{:S(2)}, u32[]{:S(2)}) %collective-permute-start.31) | collective-permute-done | bytes 131104 | tf_op jit(solution)/shard_map/ppermute | solution.py:114
  151.7 0.9 maximum_convert_fusion
  (76 shorter events, 3.6 us)
Async XLA Ops:
  0.0 121.1 %copy-start = (bf16[256,256]{1,0:T(8,128)(2,1)S(1)}, bf16[256,256]{1,0:T(8,128)(2,1)}, u32[]{:S(2)}) copy-start(bf16[256,256]{1,0:T(8,128)(2,1)} %param.10) | copy-start | bytes 393220
  0.0 13.9 %collective-permute-start = (bf16[16,16384]{1,0:T(8,128)(2,1)}, bf16[16,16384]{1,0:T(8,128)(2,1)S(1)}, u32[]{:S(2)}, u32[]{:S(2)}) collective-permute-start(bf16[16,16384]{1,0:T(8,128)(2,1)} %bitcast.57), channel_id=1, source_target_pairs={{0,32},{16,48},{32,0},{48,16},{64,96},{80,112},{96,64},{112,80},{1... | collective-permute-start | bytes 1572872 | tf_op jit(solution)/shard_map/ppermute | solution.py:256
  0.1 15.3 %collective-permute-start.1 = (bf16[16,16384]{1,0:T(8,128)(2,1)}, bf16[16,16384]{1,0:T(8,128)(2,1)S(1)}, u32[]{:S(2)}, u32[]{:S(2)}) collective-permute-start(bf16[16,16384]{1,0:T(8,128)(2,1)} %bitcast.58), channel_id=1, source_target_pairs={{0,16},{16,0},{32,48},{48,32},{64,80},{80,64},{96,112},{112,96},{1... | collective-permute-start | bytes 1572872 | tf_op jit(solution)/shard_map/ppermute | solution.py:256
  0.1 17.3 %collective-permute-start.3 = (bf16[16,16384]{1,0:T(8,128)(2,1)}, bf16[16,16384]{1,0:T(8,128)(2,1)S(1)}, u32[]{:S(2)}, u32[]{:S(2)}) collective-permute-start(bf16[16,16384]{1,0:T(8,128)(2,1)} %bitcast.59), channel_id=1, source_target_pairs={{0,64},{16,80},{32,96},{48,112},{64,128},{80,144},{96,160},{112,17... | collective-permute-start | bytes 1572872 | tf_op jit(solution)/shard_map/ppermute | solution.py:256
  1.7 15.9 %collective-permute-start.4 = (bf16[16,16384]{1,0:T(8,128)(2,1)}, bf16[16,16384]{1,0:T(8,128)(2,1)S(1)}, u32[]{:S(2)}, u32[]{:S(2)}) collective-permute-start(bf16[16,16384]{1,0:T(8,128)(2,1)} %bitcast.60), channel_id=1, source_target_pairs={{0,192},{16,208},{32,224},{48,240},{64,0},{80,16},{96,32},{112,48}... | collective-permute-start | bytes 1572872 | tf_op jit(solution)/shard_map/ppermute | solution.py:256
  13.9 4.2 %collective-permute-start.2 = (bf16[16,16384]{1,0:T(8,128)(2,1)S(1)}, bf16[16,16384]{1,0:T(8,128)(2,1)S(1)}, u32[]{:S(2)}, u32[]{:S(2)}) collective-permute-start(bf16[16,16384]{1,0:T(8,128)(2,1)S(1)} %collective-permute-done.refs_1_), channel_id=1, source_target_pairs={{0,16},{16,0},{32,48},{48,32},{64,80},{80,64},{96,112},{112,96},{1... | collective-permute-start | bytes 1572872 | tf_op jit(solution)/shard_map/ppermute | solution.py:256
  13.9 14.3 %collective-permute-start.10 = (bf16[16,16384]{1,0:T(8,128)(2,1)S(1)}, bf16[16,16384]{1,0:T(8,128)(2,1)S(1)}, u32[]{:S(2)}, u32[]{:S(2)}) collective-permute-start(bf16[16,16384]{1,0:T(8,128)(2,1)S(1)} %collective-permute-done.refs_1_), channel_id=1, source_target_pairs={{0,64},{16,80},{32,96},{48,112},{64,128},{80,144},{96,160},{112,17... | collective-permute-start | bytes 1572872 | tf_op jit(solution)/shard_map/ppermute | solution.py:256
  15.4 0.8 copy-start.2
  16.2 14.1 %collective-permute-start.11 = (bf16[16,16384]{1,0:T(8,128)(2,1)S(1)}, bf16[16,16384]{1,0:T(8,128)(2,1)S(1)}, u32[]{:S(2)}, u32[]{:S(2)}) collective-permute-start(bf16[16,16384]{1,0:T(8,128)(2,1)S(1)} %collective-permute-done.refs_1_), channel_id=1, source_target_pairs={{0,192},{16,208},{32,224},{48,240},{64,0},{80,16},{96,32},{112,48}... | collective-permute-start | bytes 1572872 | tf_op jit(solution)/shard_map/ppermute | solution.py:256
  17.5 13.3 %collective-permute-start.5 = (bf16[16,16384]{1,0:T(8,128)(2,1)S(1)}, bf16[16,16384]{1,0:T(8,128)(2,1)S(1)}, u32[]{:S(2)}, u32[]{:S(2)}) collective-permute-start(bf16[16,16384]{1,0:T(8,128)(2,1)S(1)} %collective-permute-done.3.refs_5_.refs_0_), channel_id=1, source_target_pairs={{0,16},{16,0},{32,48},{48,32},{64,80},{80,64},{96,112},{112,96},{1... | collective-permute-start | bytes 1572872 | tf_op jit(solution)/shard_map/ppermute | solution.py:256
  17.6 13.2 %collective-permute-start.6 = (bf16[16,16384]{1,0:T(8,128)(2,1)S(1)}, bf16[16,16384]{1,0:T(8,128)(2,1)S(1)}, u32[]{:S(2)}, u32[]{:S(2)}) collective-permute-start(bf16[16,16384]{1,0:T(8,128)(2,1)S(1)} %collective-permute-done.4.refs_6_.refs_1_), channel_id=1, source_target_pairs={{0,16},{16,0},{32,48},{48,32},{64,80},{80,64},{96,112},{112,96},{1... | collective-permute-start | bytes 1572872 | tf_op jit(solution)/shard_map/ppermute | solution.py:256
  18.1 0.8 copy-start.4
  18.9 1.0 copy-start.1
  19.9 1.0 copy-start.3
  21.0 1.0 copy-start.5
  22.0 0.7 copy-start.24
  30.2 5.7 %collective-permute-start.12 = (bf16[16,16384]{1,0:T(8,128)(2,1)S(1)}, bf16[16,16384]{1,0:T(8,128)(2,1)S(1)}, u32[]{:S(2)}, u32[]{:S(2)}) collective-permute-start(bf16[16,16384]{1,0:T(8,128)(2,1)S(1)} %collective-permute-done.10.refs_2_), channel_id=1, source_target_pairs={{0,16},{16,0},{32,48},{48,32},{64,80},{80,64},{96,112},{112,96},{1... | collective-permute-start | bytes 1572872 | tf_op jit(solution)/shard_map/ppermute | solution.py:256
  30.2 5.7 %collective-permute-start.13 = (bf16[16,16384]{1,0:T(8,128)(2,1)S(1)}, bf16[16,16384]{1,0:T(8,128)(2,1)S(1)}, u32[]{:S(2)}, u32[]{:S(2)}) collective-permute-start(bf16[16,16384]{1,0:T(8,128)(2,1)S(1)} %collective-permute-done.11.refs_3_), channel_id=1, source_target_pairs={{0,16},{16,0},{32,48},{48,32},{64,80},{80,64},{96,112},{112,96},{1... | collective-permute-start | bytes 1572872 | tf_op jit(solution)/shard_map/ppermute | solution.py:256
  30.7 15.2 %collective-permute-start.7 = (bf16[32,64,128]{2,1,0:T(8,128)(2,1)S(1)}, bf16[32,64,128]{2,1,0:T(8,128)(2,1)S(1)}, u32[]{:S(2)}, u32[]{:S(2)}) collective-permute-start(bf16[32,64,128]{2,1,0:T(8,128)(2,1)S(1)} %get-tuple-element.55), channel_id=1, source_target_pairs={{0,4},{1,5},{2,6},{3,7},{4,8},{5,9},{6,10},{7,11},{8,12},{9,13},{1... | collective-permute-start | bytes 1572872 | tf_op jit(solution)/shard_map/ppermute | solution.py:114
  32.3 23.1 %collective-permute-start.8 = (bf16[32,64,128]{2,1,0:T(8,128)(2,1)S(1)}, bf16[32,64,128]{2,1,0:T(8,128)(2,1)S(1)}, u32[]{:S(2)}, u32[]{:S(2)}) collective-permute-start(bf16[32,64,128]{2,1,0:T(8,128)(2,1)S(1)} %get-tuple-element.56), channel_id=1, source_target_pairs={{0,12},{1,13},{2,14},{3,15},{4,0},{5,1},{6,2},{7,3},{8,4},{9,5},{1... | collective-permute-start | bytes 1572872 | tf_op jit(solution)/shard_map/ppermute | solution.py:114
  34.0 26.5 %collective-permute-start.9 = (bf16[32,64,128]{2,1,0:T(8,128)(2,1)S(1)}, bf16[32,64,128]{2,1,0:T(8,128)(2,1)S(1)}, u32[]{:S(2)}, u32[]{:S(2)}) collective-permute-start(bf16[32,64,128]{2,1,0:T(8,128)(2,1)S(1)} %get-tuple-element.57), channel_id=1, source_target_pairs={{0,8},{1,9},{2,10},{3,11},{4,12},{5,13},{6,14},{7,15},{8,0},{9,1},... | collective-permute-start | bytes 1572872 | tf_op jit(solution)/shard_map/ppermute | solution.py:114
  36.0 25.3 %collective-permute-start.17 = (bf16[16,16384]{1,0:T(8,128)(2,1)S(1)}, bf16[16,16384]{1,0:T(8,128)(2,1)S(1)}, u32[]{:S(2)}, u32[]{:S(2)}) collective-permute-start(bf16[16,16384]{1,0:T(8,128)(2,1)S(1)} %collective-permute-done.3.refs_5_.refs_0_), channel_id=1, source_target_pairs={{0,64},{16,80},{32,96},{48,112},{64,128},{80,144},{96,160},{112,17... | collective-permute-start | bytes 1572872 | tf_op jit(solution)/shard_map/ppermute | solution.py:256
  37.2 24.1 %collective-permute-start.18 = (bf16[16,16384]{1,0:T(8,128)(2,1)S(1)}, bf16[16,16384]{1,0:T(8,128)(2,1)S(1)}, u32[]{:S(2)}, u32[]{:S(2)}) collective-permute-start(bf16[16,16384]{1,0:T(8,128)(2,1)S(1)} %collective-permute-done.11.refs_3_), channel_id=1, source_target_pairs={{0,192},{16,208},{32,224},{48,240},{64,0},{80,16},{96,32},{112,48}... | collective-permute-start | bytes 1572872 | tf_op jit(solution)/shard_map/ppermute | solution.py:256
  38.0 39.8 %copy-start.25 = (s32[1,1,192,2]{2,3,1,0:T(2,128)S(1)}, s32[1,1,192,2]{2,3,1,0:T(2,128)}, u32[]{:S(2)}) copy-start(s32[1,1,192,2]{2,3,1,0:T(2,128)} %param.8) | copy-start | bytes 4612
  43.2 0.8 copy-start.10
  44.0 0.8 copy-start.12
  45.9 52.4 %copy-start.11 = (bf16[16,128,128]{2,1,0:T(8,128)(2,1)S(1)}, bf16[16,128,128]{2,1,0:T(8,128)(2,1)}, u32[]{:S(2)}) copy-start(bf16[16,128,128]{2,1,0:T(8,128)(2,1)} %copy-done.10) | copy-start | bytes 1572868
  45.9 23.6 %collective-permute-start.14 = (bf16[16,128,128]{2,1,0:T(8,128)(2,1)S(1)}, bf16[16,128,128]{2,1,0:T(8,128)(2,1)S(1)}, u32[]{:S(2)}, u32[]{:S(2)}) collective-permute-start(bf16[16,128,128]{2,1,0:T(8,128)(2,1)S(1)} %get-tuple-element.67), channel_id=1, source_target_pairs={{0,4},{1,5},{2,6},{3,7},{4,8},{5,9},{6,10},{7,11},{8,12},{9,13},{1... | collective-permute-start | bytes 1572872 | tf_op jit(solution)/shard_map/ppermute | solution.py:114
  55.5 0.8 copy-start.6
  56.3 42.0 %copy-start.7 = (bf16[32,64,128]{2,1,0:T(8,128)(2,1)S(1)}, bf16[32,64,128]{2,1,0:T(8,128)(2,1)}, u32[]{:S(2)}) copy-start(bf16[32,64,128]{2,1,0:T(8,128)(2,1)} %copy-done.6) | copy-start | bytes 1572868
  56.3 13.3 %collective-permute-start.15 = (bf16[16,128,128]{2,1,0:T(8,128)(2,1)S(1)}, bf16[16,128,128]{2,1,0:T(8,128)(2,1)S(1)}, u32[]{:S(2)}, u32[]{:S(2)}) collective-permute-start(bf16[16,128,128]{2,1,0:T(8,128)(2,1)S(1)} %get-tuple-element.68), channel_id=1, source_target_pairs={{0,12},{1,13},{2,14},{3,15},{4,0},{5,1},{6,2},{7,3},{8,4},{9,5},{1... | collective-permute-start | bytes 1572872 | tf_op jit(solution)/shard_map/ppermute | solution.py:114
  60.5 0.8 copy-start.8
  61.2 37.1 %copy-start.9 = (bf16[32,64,128]{2,1,0:T(8,128)(2,1)S(1)}, bf16[32,64,128]{2,1,0:T(8,128)(2,1)}, u32[]{:S(2)}) copy-start(bf16[32,64,128]{2,1,0:T(8,128)(2,1)} %copy-done.8) | copy-start | bytes 1572868
  61.3 37.1 %copy-start.13 = (bf16[16,128,128]{2,1,0:T(8,128)(2,1)S(1)}, bf16[16,128,128]{2,1,0:T(8,128)(2,1)}, u32[]{:S(2)}) copy-start(bf16[16,128,128]{2,1,0:T(8,128)(2,1)} %copy-done.12) | copy-start | bytes 1572868
  61.3 12.7 %collective-permute-start.19 = (bf16[16,16384]{1,0:T(8,128)(2,1)S(1)}, bf16[16,16384]{1,0:T(8,128)(2,1)S(1)}, u32[]{:S(2)}, u32[]{:S(2)}) collective-permute-start(bf16[16,16384]{1,0:T(8,128)(2,1)S(1)} %collective-permute-done.17.refs_0_), channel_id=1, source_target_pairs={{0,16},{16,0},{32,48},{48,32},{64,80},{80,64},{96,112},{112,96},{1... | collective-permute-start | bytes 1572872 | tf_op jit(solution)/shard_map/ppermute | solution.py:256
  61.4 0.8 copy-start.14
  62.2 12.6 %collective-permute-start.20 = (bf16[16,16384]{1,0:T(8,128)(2,1)S(1)}, bf16[16,16384]{1,0:T(8,128)(2,1)S(1)}, u32[]{:S(2)}, u32[]{:S(2)}) collective-permute-start(bf16[16,16384]{1,0:T(8,128)(2,1)S(1)} %collective-permute-done.18.refs_1_), channel_id=1, source_target_pairs={{0,16},{16,0},{32,48},{48,32},{64,80},{80,64},{96,112},{112,96},{1... | collective-permute-start | bytes 1572872 | tf_op jit(solution)/shard_map/ppermute | solution.py:256
  62.7 0.8 copy-start.16
  70.7 17.1 %collective-permute-start.16 = (bf16[16,128,128]{2,1,0:T(8,128)(2,1)}, bf16[16,128,128]{2,1,0:T(8,128)(2,1)}, u32[]{:S(2)}, u32[]{:S(2)}) collective-permute-start(bf16[16,128,128]{2,1,0:T(8,128)(2,1)} %get-tuple-element.69.refs_5_), channel_id=1, source_target_pairs={{0,4},{1,5},{2,6},{3,7},{4,8},{5,9},{6,10},{7,11},{8,12},{9,13},{1... | collective-permute-start | bytes 1572872 | tf_op jit(solution)/shard_map/ppermute | solution.py:114
  71.9 18.4 %collective-permute-start.23 = (bf16[16,128,128]{2,1,0:T(8,128)(2,1)}, bf16[16,128,128]{2,1,0:T(8,128)(2,1)}, u32[]{:S(2)}, u32[]{:S(2)}) collective-permute-start(bf16[16,128,128]{2,1,0:T(8,128)(2,1)} %get-tuple-element.77.refs_6_), channel_id=1, source_target_pairs={{0,12},{1,13},{2,14},{3,15},{4,0},{5,1},{6,2},{7,3},{8,4},{9,5},{1... | collective-permute-start | bytes 1572872 | tf_op jit(solution)/shard_map/ppermute | solution.py:114
  74.0 0.8 copy-start.18
  74.8 0.8 copy-start.20
  75.7 22.6 %collective-permute-start.21 = (bf16[16,128,128]{2,1,0:T(8,128)(2,1)}, bf16[16,128,128]{2,1,0:T(8,128)(2,1)}, u32[]{:S(2)}, u32[]{:S(2)}) collective-permute-start(bf16[16,128,128]{2,1,0:T(8,128)(2,1)} %get-tuple-element.75), channel_id=1, source_target_pairs={{0,12},{1,13},{2,14},{3,15},{4,0},{5,1},{6,2},{7,3},{8,4},{9,5},{1... | collective-permute-start | bytes 1572872 | tf_op jit(solution)/shard_map/ppermute | solution.py:114
  76.3 22.0 %collective-permute-start.22 = (bf16[16,128,128]{2,1,0:T(8,128)(2,1)}, bf16[16,128,128]{2,1,0:T(8,128)(2,1)}, u32[]{:S(2)}, u32[]{:S(2)}) collective-permute-start(bf16[16,128,128]{2,1,0:T(8,128)(2,1)} %get-tuple-element.76), channel_id=1, source_target_pairs={{0,4},{1,5},{2,6},{3,7},{4,8},{5,9},{6,10},{7,11},{8,12},{9,13},{1... | collective-permute-start | bytes 1572872 | tf_op jit(solution)/shard_map/ppermute | solution.py:114
  77.8 1.0 copy-start.15
  78.8 1.0 copy-start.17
  79.9 1.0 copy-start.19
  80.9 1.0 copy-start.21
  86.9 14.2 %copy-start.22 = (bf16[32,64,128]{2,1,0:T(8,128)(2,1)}, bf16[32,64,128]{2,1,0:T(8,128)(2,1)S(1)}, u32[]{:S(2)}) copy-start(bf16[32,64,128]{2,1,0:T(8,128)(2,1)S(1)} %get-tuple-element.85) | copy-start | bytes 1572868
  86.9 52.6 %copy-start.26 = (f32[256]{0:T(256)S(1)}, f32[256]{0:T(256)}, u32[]{:S(2)}) copy-start(f32[256]{0:T(256)} %param.11) | copy-start | bytes 3076
  86.9 35.4 %collective-permute-start.28 = (bf16[32,64,128]{2,1,0:T(8,128)(2,1)}, bf16[32,64,128]{2,1,0:T(8,128)(2,1)}, u32[]{:S(2)}, u32[]{:S(2)}) collective-permute-start(bf16[32,64,128]{2,1,0:T(8,128)(2,1)} %get-tuple-element.86), channel_id=1, source_target_pairs={{0,4},{1,5},{2,6},{3,7},{4,8},{5,9},{6,10},{7,11},{8,12},{9,13},{1... | collective-permute-start | bytes 1572872 | tf_op jit(solution)/shard_map/ppermute | solution.py:114
  87.9 34.4 %collective-permute-start.29 = (bf16[32,64,128]{2,1,0:T(8,128)(2,1)}, bf16[32,64,128]{2,1,0:T(8,128)(2,1)}, u32[]{:S(2)}, u32[]{:S(2)}) collective-permute-start(bf16[32,64,128]{2,1,0:T(8,128)(2,1)} %get-tuple-element.87), channel_id=1, source_target_pairs={{0,12},{1,13},{2,14},{3,15},{4,0},{5,1},{6,2},{7,3},{8,4},{9,5},{1... | collective-permute-start | bytes 1572872 | tf_op jit(solution)/shard_map/ppermute | solution.py:114
  90.2 32.1 %collective-permute-start.30 = (bf16[32,64,128]{2,1,0:T(8,128)(2,1)}, bf16[32,64,128]{2,1,0:T(8,128)(2,1)}, u32[]{:S(2)}, u32[]{:S(2)}) collective-permute-start(bf16[32,64,128]{2,1,0:T(8,128)(2,1)} %get-tuple-element.88), channel_id=1, source_target_pairs={{0,8},{1,9},{2,10},{3,11},{4,12},{5,13},{6,14},{7,15},{8,0},{9,1},... | collective-permute-start | bytes 1572872 | tf_op jit(solution)/shard_map/ppermute | solution.py:114
  101.1 0.8 copy-start.23
  101.9 13.4 %collective-permute-start.24 = (bf16[4,192,128]{2,1,0:T(8,128)(2,1)}, bf16[4,192,128]{2,1,0:T(8,128)(2,1)S(1)}, u32[]{:S(2)}, u32[]{:S(2)}) collective-permute-start(bf16[4,192,128]{2,1,0:T(8,128)(2,1)} %get-tuple-element.81), channel_id=1, source_target_pairs={{0,1},{1,2},{2,3},{3,0},{4,5},{5,6},{6,7},{7,4},{8,9},{9,10},{10,1... | collective-permute-start | bytes 589832 | tf_op jit(solution)/shard_map/ppermute | solution.py:114
  105.1 10.1 %collective-permute-start.25 = (bf16[4,192,128]{2,1,0:T(8,128)(2,1)S(1)}, bf16[4,192,128]{2,1,0:T(8,128)(2,1)S(1)}, u32[]{:S(2)}, u32[]{:S(2)}) collective-permute-start(bf16[4,192,128]{2,1,0:T(8,128)(2,1)S(1)} %get-tuple-element.82), channel_id=1, source_target_pairs={{0,3},{1,0},{2,1},{3,2},{4,7},{5,4},{6,5},{7,6},{8,11},{9,8},{10,9... | collective-permute-start | bytes 589832 | tf_op jit(solution)/shard_map/ppermute | solution.py:114
  117.1 20.0 %collective-permute-start.27 = (bf16[8,192,128]{2,1,0:T(8,128)(2,1)}, bf16[8,192,128]{2,1,0:T(8,128)(2,1)S(1)}, u32[]{:S(2)}, u32[]{:S(2)}) collective-permute-start(bf16[8,192,128]{2,1,0:T(8,128)(2,1)} %get-tuple-element.84), channel_id=1, source_target_pairs={{0,3},{1,0},{2,1},{3,2},{4,7},{5,4},{6,5},{7,6},{8,11},{9,8},{10,9... | collective-permute-start | bytes 1179656 | tf_op jit(solution)/shard_map/ppermute | solution.py:114
  119.7 19.8 %collective-permute-start.26 = (bf16[8,192,128]{2,1,0:T(8,128)(2,1)}, bf16[8,192,128]{2,1,0:T(8,128)(2,1)S(1)}, u32[]{:S(2)}, u32[]{:S(2)}) collective-permute-start(bf16[8,192,128]{2,1,0:T(8,128)(2,1)} %get-tuple-element.83), channel_id=1, source_target_pairs={{0,1},{1,2},{2,3},{3,0},{4,5},{5,6},{6,7},{7,4},{8,9},{9,10},{10,1... | collective-permute-start | bytes 1179656 | tf_op jit(solution)/shard_map/ppermute | solution.py:114
  124.3 27.1 %collective-permute-start.31 = (bf16[8,64,128]{2,1,0:T(8,128)(2,1)S(1)}, bf16[8,64,128]{2,1,0:T(8,128)(2,1)S(1)}, u32[]{:S(2)}, u32[]{:S(2)}) collective-permute-start(bf16[8,64,128]{2,1,0:T(8,128)(2,1)S(1)} %get-tuple-element.99), channel_id=1, source_target_pairs={{0,1},{1,2},{2,3},{3,0},{4,5},{5,6},{6,7},{7,4},{8,9},{9,10},{10,1... | collective-permute-start | bytes 393224 | tf_op jit(solution)/shard_map/ppermute | solution.py:114
  128.5 22.9 %collective-permute-start.32 = (bf16[8,64,128]{2,1,0:T(8,128)(2,1)S(1)}, bf16[8,64,128]{2,1,0:T(8,128)(2,1)S(1)}, u32[]{:S(2)}, u32[]{:S(2)}) collective-permute-start(bf16[8,64,128]{2,1,0:T(8,128)(2,1)S(1)} %get-tuple-element.98), channel_id=1, source_target_pairs={{0,2},{1,3},{2,0},{3,1},{4,6},{5,7},{6,4},{7,5},{8,10},{9,11},{10,... | collective-permute-start | bytes 393224 | tf_op jit(solution)/shard_map/ppermute | solution.py:114
  131.4 20.0 %collective-permute-start.33 = (bf16[8,64,128]{2,1,0:T(8,128)(2,1)S(1)}, bf16[8,64,128]{2,1,0:T(8,128)(2,1)S(1)}, u32[]{:S(2)}, u32[]{:S(2)}) collective-permute-start(bf16[8,64,128]{2,1,0:T(8,128)(2,1)S(1)} %get-tuple-element.97), channel_id=1, source_target_pairs={{0,3},{1,0},{2,1},{3,2},{4,7},{5,4},{6,5},{7,6},{8,11},{9,8},{10,9... | collective-permute-start | bytes 393224 | tf_op jit(solution)/shard_map/ppermute | solution.py:114
